TPU v7x, 256 devices: a whole 4x4x8 slice. The times are simulated.
256 devices in a mesh: dp: 32 (over y, x, core), mp: 8 (over z).
Axes of the slice: x: 4, y: 4, z: 8, core: 2. Of those that a mesh axis runs over, the one named last changes fastest.
Arguments:
- feats: bfloat16 [32768, 2048], P('dp', 'mp'), may hold values from -6 to 6
- parent: int32 [32768], P('dp'), may hold values from 0 to 1022, as said below
- counts: int32 [32], replicated, may hold values from 1 to 1024, 16384 in all
- accepted: int32 [32768], P('dp'), may hold values 0 or 1
- cand_ids: int32 [32768, 8], P('dp'), may hold values from 0 to 128255, as said below
- target_probs: bfloat16 [32768, 8], P('dp'), may hold values from 0 to 1, as said below
- gain: bfloat16 [2048], P('mp'), may hold values from 0.5 to 2
- embed: bfloat16 [128256, 2048], P('dp', 'mp'), may hold values from -0.125 to 0.125
- proj: bfloat16 [2048, 2048], P(None, 'mp'), may hold values from -6 to 6
Outputs:
- new_proj: bfloat16 [2048, 2048], P(None, 'mp')
- loss: float32 [], replicated
Inputs may be any that keep to these rules, and one draw needn't show every extreme that they name: parent of a row with local index i is a local index below i; the row of local index 0 names 0, and the row of local index 1023 names 1022. `cand_ids`: among the 8192 candidates of one group, at most 384 lie in any one block of 4008 consecutive ids starting at a multiple of 4008, and in every group some block holds exactly 384. `target_probs`: positive.
All inputs are finite; a program needn't handle non-finite values. No bound on the sum of `accepted` on one device may be relied on, other than what follows from the above.
Results may differ from a plain program's by a relative error of at most 0.008.
Values may be sent and summed in bfloat16 or wider, within the bound.
A program may use at most 128 MiB of HBM per device.

v0:
```python
import functools
import jax
import jax.numpy as jnp
from jax import lax
from jax.experimental import pallas as pl
from jax.experimental.pallas import tpu as pltpu
from jax.sharding import PartitionSpec as P

MESH = pl.DeviceIdType.MESH
F32 = jnp.float32
BF16 = jnp.bfloat16
I32 = jnp.int32

GROUP = 4
CAP = 352
CAPL = 384
HALF = 224


def dot(a, b):
    return jnp.dot(a, b, preferred_element_type=F32)


def dot_nt(a, b):
    return lax.dot_general(a, b, (((1,), (1,)), ((), ())), preferred_element_type=F32)


def one_hot(hit):
    return jnp.where(hit, 1.0, 0.0).astype(BF16)


def iota(shape, axis):
    return lax.broadcasted_iota(I32, shape, axis)


def step_kernel(
    nd, nz, full_rows,
    counts, ids, odds, parent, accepted, feats, gain, embed, proj,
    out, stat,
    emb, perm, meta, metap, metar, mixp, mixr, live, metat,
    sendid, idr, rows_out, rows_in, whole, whole_t, hidden, ng,
    pick, pick_t, kmat, ksel, sc, zsend, zr, scaled, dn, dh,
    pair_out, pair_in, gown, rs_out, rs_in, gfull, ez_out, ez, dt_out, dt,
    emb_s, emb_r, meta_s, meta_r, mix_s, mix_r, id_s, id_r, row_s, row_r,
    zr_s, zr_r, zl_s, zl_r, zx_s, zx_r, pair_s, pair_r,
    rs_s, rs_r, ag_s, ag_r, fw_s, fw_r, ez_s, ez_r, dt_s, dt_r,
):
    me = lax.axis_index("dp")
    z = lax.axis_index("mp")
    nodes = feats.shape[0]
    width = feats.shape[1]
    slots = live.shape[0]
    share = nodes // nd
    core = lax.rem(me, 2)
    chip = lax.div(me, 2)
    chips = nd // 2
    sibling = me + 1 - 2 * core
    vocab = embed.shape[0]

    sent = []

    def copy(src, dst, ss, rs, d, zz):
        return pltpu.make_async_remote_copy(
            src_ref=src, dst_ref=dst, send_sem=ss, recv_sem=rs,
            device_id=(d, zz), device_id_type=MESH,
        )

    def nxt(i):
        return lax.rem(me + i, nd)

    def prv(i):
        return lax.rem(me - i + nd, nd)

    def loop(lo, hi, body):
        def wrapped(i, carry):
            body(i)
            return carry
        lax.fori_loop(lo, hi, wrapped, 0)

    def dp_copy(src, dst, ss, rs, d):
        return copy(src.at[d], dst.at[me], ss.at[d], rs.at[me], d, z)

    def dp_wait(src, dst, ss, rs, h):
        copy(src.at[h], dst.at[h], ss.at[h], rs.at[h], h, z).wait_recv()

    def dp_send_all(src, dst, ss, rs):
        loop(1, nd, lambda i: dp_copy(src, dst, ss, rs, nxt(i)).start())
        sent.append(lambda: dp_sent_all(src, dst, ss, rs))

    def dp_wait_all(src, dst, ss, rs):
        loop(1, nd, lambda i: dp_wait(src, dst, ss, rs, prv(i)))

    def dp_sent_all(src, dst, ss, rs):
        loop(1, nd, lambda i: dp_copy(src, dst, ss, rs, nxt(i)).wait_send())

    side = int(chips ** 0.5)
    chip_x = lax.rem(chip, side)
    chip_y = lax.div(chip, side)

    def offset(i):
        dx = lax.rem(i, side)
        dy = lax.rem(lax.div(i, side) + i, side)
        return dx + core * (dy - dx), dy + core * (dx - dy)

    def to_chip(i):
        dx, dy = offset(i)
        return lax.rem(chip_y + dy, side) * side + lax.rem(chip_x + dx, side)

    def from_chip(i):
        dx, dy = offset(i)
        return lax.rem(chip_y - dy + side, side) * side + lax.rem(chip_x - dx + side, side)

    def chip_copy(src, dst, ss, rs, p):
        return copy(src.at[p], dst.at[chip], ss.at[p], rs.at[chip], p * 2 + core, z)

    def chip_wait(src, dst, ss, rs, p):
        copy(src.at[p], dst.at[p], ss.at[p], rs.at[p], p * 2 + core, z).wait_recv()

    def chip_sent_all(src, dst, ss, rs):
        loop(1, chips, lambda i: chip_copy(src, dst, ss, rs, to_chip(i)).wait_send())

    barrier = pltpu.get_barrier_semaphore()
    loop(1, nd, lambda i: pl.semaphore_signal(barrier, inc=1, device_id=(nxt(i), z), device_id_type=MESH))
    loop(1, nz, lambda i: pl.semaphore_signal(barrier, inc=1, device_id=(me, lax.rem(z + i, nz)), device_id_type=MESH))

    node_lane = iota((1, nodes), 1)
    lane_h = lax.div(node_lane, share)
    lane_j = node_lane - lane_h * share

    def deal(h, state):
        off, mine, into = state
        count = counts[h]
        first = (me - off) & (nd - 1)
        base = (off + first) // nd
        row = jnp.where(lane_j * nd + first < count, base + lane_j, -1)
        return off + count, jnp.where(h == me, off, mine), jnp.where(lane_h == h, row, into)

    _, mine, into = lax.fori_loop(
        0, nd, deal, (jnp.int32(0), jnp.int32(0), jnp.full((1, nodes), -1, I32))
    )
    dealt = ((node_lane + mine) & (nd - 1)) * share + lax.div(node_lane, nd)

    def in_row(ref):
        return jnp.concatenate([ref[r:r + 1, :] for r in range(ref.shape[0])], axis=1)

    idf = ids[...].astype(F32)
    own_f = jnp.floor((idf + 0.5) * (1.0 / float(vocab)))
    at_f = idf - own_f * float(vocab)
    hi_f = jnp.floor(at_f * (1.0 / 256.0))
    par = in_row(parent)
    extra = jnp.concatenate(
        [
            in_row(accepted).astype(F32),
            (par // 32).astype(F32),
            (par % 32).astype(F32),
            jnp.zeros((5, nodes), F32),
        ],
        axis=0,
    )
    table = jnp.concatenate(
        [own_f, hi_f + 1.0, at_f - 256.0 * hi_f, odds[...].astype(F32), extra, jnp.zeros((88, nodes), F32)],
        axis=0,
    )
    meta[...] = table.T.astype(BF16)

    step = 128

    def perm_block(b):
        rows = pl.ds(b * step, step)
        e = one_hot(iota((step, nodes), 0) + b * step == dealt)
        perm[rows, :] = e
        metap[pl.ds(b * (step // share), step // share)] = (
            dot(e, meta[...]).astype(BF16).reshape(step // share, share, metap.shape[2])
        )

    loop(0, nodes // step, perm_block)

    block = emb.shape[1]
    even = vocab // 32 * 32
    emb[core, 0:even, :] = embed[0:even, :]
    emb[core, even:block, :] = jnp.concatenate(
        [embed[even:vocab, :].astype(F32), jnp.zeros((block - vocab, width), F32)], axis=0
    ).astype(BF16)
    pl.semaphore_wait(barrier, nd - 1 + nz - 1)

    def emb_copy(c):
        return copy(emb.at[c], emb.at[c], emb_s.at[c], emb_r.at[c], sibling, z)

    emb_copy(core).start()
    sent.append(lambda: emb_copy(core).wait_send())
    dp_send_all(metap, metar, meta_s, meta_r)
    metar[me] = metap[me]

    def mixp_block(b):
        mine_b = metap[pl.ds(b * (step // share), step // share)].reshape(step, metap.shape[2]).astype(F32)
        at = mine_b[:, 33:34] * 32.0 + mine_b[:, 34:35]
        p = one_hot(iota((step, nodes), 1) == at.astype(I32))
        mixp[pl.ds(b * (step // share), step // share)] = (
            dot(perm[pl.ds(b * step, step), :] + p, feats[...])
            .astype(BF16)
            .reshape(step // share, share, width)
        )

    loop(0, nodes // step, mixp_block)
    dp_send_all(mixp, mixr, mix_s, mix_r)
    mixr[me] = mixp[me]

    def live_block(b):
        live[pl.ds(b * step, step), :] = one_hot(iota((step, nodes), 0) + b * step == into)

    loop(0, slots // step, live_block)

    dp_wait_all(metap, metar, meta_s, meta_r)
    for b in range(slots // step):
        part = dot(live[b * step:(b + 1) * step, :], metar[...].reshape(nodes, metar.shape[2]))
        metat[:, b * step:(b + 1) * step] = part.T

    owner = metat[0:8, :].astype(I32)
    upper = one_hot(iota((slots, slots), 0) < iota((slots, slots), 1))
    own_iota = iota((nd, slots), 0)
    member = jnp.concatenate(
        [jnp.where(own_iota == owner[k:k + 1, :], 1.0, 0.0) for k in range(8)], axis=0
    )
    before = dot(member.astype(BF16), upper)
    carry = jnp.zeros((nd, 1), F32)
    lists = jnp.zeros((chips * 8, CAPL), F32)
    asks = jnp.zeros((chips, 1), F32)
    at_chip = owner // 2
    odd_core = owner - 2 * at_chip
    chip_iota = iota((chips, slots), 0)
    node_row = iota((1, slots), 1)
    for k in range(8):
        mk = member[k * nd:(k + 1) * nd, :]
        rank = jnp.sum(mk * (before[k * nd:(k + 1) * nd, :] + carry), axis=0, keepdims=True)
        carry = carry + jnp.sum(mk, axis=1, keepdims=True)
        odd_k = odd_core[k:k + 1, :].astype(F32)
        place = rank + odd_k * (float(CAP - 1) - 2.0 * rank)
        asks = asks + jnp.sum(jnp.where(chip_iota == at_chip[k:k + 1, :], 1.0, 0.0), axis=1, keepdims=True)
        fields = jnp.concatenate(
            [
                metat[8 + k:9 + k, :] + float(block // 256) * odd_k,
                metat[16 + k:17 + k, :],
                (node_row // 2).astype(F32),
                ((node_row % 2) * 8 + (k + 1)).astype(F32),
                jnp.zeros((4, slots), F32),
            ],
            axis=0,
        )
        here = iota((chips, 8, slots), 0) == at_chip[k:k + 1, :][None]
        f = jnp.where(here, fields[None], 0.0).reshape(chips * 8, slots).astype(BF16)
        at = one_hot(iota((CAPL, slots), 0) == place.astype(I32))
        lists = lists + dot_nt(f, at)
    sendid[...] = lists.reshape(chips, 8, CAPL)
    over = jnp.maximum(
        jnp.max(jnp.where(carry > float(HALF), 1.0, 0.0), axis=0, keepdims=True),
        jnp.max(jnp.where(asks > float(CAP), 1.0, 0.0), axis=0, keepdims=True),
    )
    loop(1, chips, lambda i: chip_copy(sendid, idr, id_s, id_r, to_chip(i)).start())
    sent.append(lambda: chip_sent_all(sendid, idr, id_s, id_r))
    idr[chip] = sendid[chip]

    dp_wait_all(mixp, mixr, mix_s, mix_r)
    for b in range(slots // step):
        part = dot(live[b * step:(b + 1) * step, :], mixr[...].reshape(nodes, width))
        whole[z, b * step:(b + 1) * step, :] = part.astype(BF16)
    zright = lax.rem(z + 1, nz)
    zleft = lax.rem(z + nz - 1, nz)

    def ring_right(s):
        b = lax.rem(z - s + nz, nz)
        return copy(whole.at[b], whole.at[b], zr_s.at[s], zr_r.at[s], me, zright)

    def ring_left(s):
        b = lax.rem(z + s, nz)
        return copy(whole.at[b], whole.at[b], zl_s.at[s], zl_r.at[s], me, zleft)

    def got_right(s):
        b = lax.rem(z - s - 1 + nz, nz)
        copy(whole.at[b], whole.at[b], zr_s.at[s], zr_r.at[s], me, zright).wait_recv()
        return b

    def got_left(s):
        b = lax.rem(z + s + 1, nz)
        copy(whole.at[b], whole.at[b], zl_s.at[s], zl_r.at[s], me, zleft).wait_recv()
        return b

    n_right = nz // 2
    n_left = nz - 1 - n_right
    ring_right(0).start()
    ring_left(0).start()

    scale = 1.0 / (float(full_rows) ** 0.5)

    def use_block(b, first=False):
        blk = whole[b]
        whole_t[b] = blk.T
        h = dot(blk, proj[pl.ds(pl.multiple_of(b * width, width), width), :])
        if first:
            hidden[...] = h
        else:
            hidden[...] += h

    chunk = 256

    low = CAP - HALF

    def serve(h):
        cols = idr[h].T
        hi = jnp.broadcast_to(cols[:CAP, 0:1], (CAP, chunk)).astype(BF16)
        lo = one_hot(iota((CAP, chunk), 1) == cols[:CAP, 1:2].astype(I32))
        halves = []
        for c in range(2):
            first = c * low
            parts = [
                jnp.where(
                    hi[first:first + HALF, :] == jnp.bfloat16(c * (block // chunk) + i + 1),
                    lo[first:first + HALF, :],
                    jnp.bfloat16(0),
                )
                for i in range(block // chunk)
            ]
            halves.append(dot(jnp.concatenate(parts, axis=1), emb[c]))
        front, rear = halves
        rows_out[h, 0:low, :] = front[0:low, :].astype(BF16)
        rows_out[h, low:HALF, :] = (front[low:, :] + rear[:HALF - low, :]).astype(BF16)
        rows_out[h, HALF:CAP, :] = rear[HALF - low:, :].astype(BF16)

    def serve_far(i):
        h = to_chip(i)
        chip_wait(sendid, idr, id_s, id_r, h)
        serve(h)
        chip_copy(rows_out, rows_in, row_s, row_r, h).start()

    emb_copy(1 - core).wait_recv()
    use_block(z, True)
    done = 1
    plan = [(4, 0), (7, 1), (10, 2), (13, 3)]
    for upto, s in plan:
        loop(done, upto, serve_far)
        done = upto
        if s < n_right:
            b = got_right(s)
            if s + 1 < n_right:
                ring_right(s + 1).start()
            use_block(b)
        if s < n_left:
            b = got_left(s)
            if s + 1 < n_left:
                ring_left(s + 1).start()
            use_block(b)
    loop(done, chips, serve_far)
    serve(chip)
    rows_in[chip] = rows_out[chip]
    sent.append(lambda: chip_sent_all(rows_out, rows_in, row_s, row_r))
    for s in range(n_right):
        sent.append(functools.partial(lambda s: ring_right(s).wait_send(), s))
    for s in range(n_left):
        sent.append(functools.partial(lambda s: ring_left(s).wait_send(), s))

    hid = hidden[...] * scale
    hidden[...] = hid
    square = jnp.sum(hid * hid, axis=1, keepdims=True)
    ng[...] = (hid * gain[...].astype(F32)).astype(BF16)
    lane = iota((slots, 128), 1)
    sc[...] = jnp.where(lane == 16, square, 0.0)
    kmat[...] = jnp.zeros(kmat.shape, BF16)
    scaled[...] = jnp.zeros(scaled.shape, BF16)

    def unpack(a, b):
        bm = b - 1.0
        odd = jnp.where(bm >= 8.0, 1.0, 0.0)
        k = jnp.where(b > 0.0, bm - 8.0 * odd, -1.0)
        node = jnp.where(b > 0.0, 2.0 * a + odd, -1.0)
        return node.astype(I32), k.astype(I32)

    def owner_at(j, q):
        return from_chip(j * GROUP + q + 1)

    def score(j):
        for q in range(GROUP):
            lists_o = sendid[owner_at(j, q)]
            cols = lists_o.T
            node_c, k_c = unpack(cols[:CAP, 2:3], cols[:CAP, 3:4])
            node_r, _ = unpack(lists_o[2:3, :], lists_o[3:4, :])
            pick[j, q * CAP:(q + 1) * CAP, :] = one_hot(iota((CAP, slots), 1) == node_c)
            pick_t[j, :, q * CAPL:(q + 1) * CAPL] = one_hot(iota((slots, CAPL), 0) == node_r)
            ln = iota((CAP, 128), 1)
            ksel[j, q * CAP:(q + 1) * CAP, :] = one_hot(ln == k_c) + one_hot((ln == k_c + 8) & (k_c >= 0))
        for q in range(GROUP):
            wait_rows(j, q)
        asked = dot(pick[j], ng[...])
        for q in range(GROUP):
            got = rows_in[owner_at(j, q)].astype(F32)
            s = jnp.sum(got * asked[q * CAP:(q + 1) * CAP, :], axis=1, keepdims=True)
            s_hi = s.astype(BF16).astype(F32)
            ln = iota((CAP, 128), 1)
            val = jnp.where(ln < 8, s_hi, s - s_hi) * ksel[j, q * CAP:(q + 1) * CAP, :].astype(F32)
            kmat[q * CAPL:q * CAPL + CAP, :] = val.astype(BF16)
        sc[...] += dot(pick_t[j], kmat[...])

    def wait_rows(j, q):
        chip_wait(rows_out, rows_in, row_s, row_r, owner_at(j, q))

    groups = chips // GROUP
    loop(0, groups - 1, score)
    last = groups - 1

    def wait_rows(j, q):
        if q + 1 < GROUP:
            chip_wait(rows_out, rows_in, row_s, row_r, owner_at(j, q))

    score(last)

    sct = sc[...].T
    zsend[0:8, :] = sct[0:8, :] + sct[8:16, :]
    zsend[8:16, :] = sct[16:24, :]

    def zx(i):
        zz = lax.rem(z + i, nz)
        return copy(zsend, zr.at[z], zx_s.at[zz], zx_r.at[z], me, zz)

    def zx_wait(i):
        zz = lax.rem(z + i, nz)
        copy(zsend, zr.at[zz], zx_s.at[zz], zx_r.at[zz], me, zz).wait_recv()

    loop(1, nz, lambda i: zx(i).start())
    sent.append(lambda: loop(1, nz, lambda i: zx(i).wait_send()))
    zr[z] = zsend[...]
    loop(1, nz, zx_wait)
    tot = zr[0]
    for i in range(1, nz):
        tot = tot + zr[i]
    raw = tot[0:8, :]
    recip = lax.rsqrt(tot[8:9, :] / float(full_rows) + 1e-05)
    scores = raw * recip
    logp = scores - jnp.log(jnp.sum(jnp.exp(scores), axis=0, keepdims=True))
    prob = jnp.exp(logp)
    probs = metat[24:32, :]
    target = probs / jnp.sum(probs, axis=0, keepdims=True)
    kl = jnp.sum(target * (jnp.log(target) - logp), axis=0, keepdims=True)
    weight = 1.0 + metat[32:33, :]
    num = jnp.sum(weight * kl, axis=1, keepdims=True)
    den = jnp.sum(weight, axis=1, keepdims=True)
    gs = weight * (prob - target)
    inner = jnp.sum(gs * raw, axis=0, keepdims=True)
    back = recip * recip * recip * inner * (1.0 / float(full_rows))
    gs_hi = gs.astype(BF16).astype(F32)
    gs16 = jnp.concatenate([gs_hi, gs - gs_hi], axis=0).astype(BF16)
    coef = jnp.concatenate([recip, back, jnp.zeros((6, slots), F32)], axis=0).T
    dn[...] = jnp.zeros(dn.shape, F32)

    def spread(j):
        g16 = dot_nt(pick[j], gs16)
        g = jnp.sum(g16 * ksel[j][:, 0:16].astype(F32), axis=1, keepdims=True)
        for q in range(GROUP):
            got = rows_in[owner_at(j, q)].astype(F32)
            scaled[q * CAPL:q * CAPL + CAP, :] = (got * g[q * CAP:(q + 1) * CAP, :]).astype(BF16)
        dn[...] += dot(pick_t[j], scaled[...])

    loop(0, groups, spread)
    dh[...] = (coef[:, 0:1] * gain[...].astype(F32) * dn[...] - hidden[...] * coef[:, 1:2]).astype(BF16)

    quarter = nz // 2

    def pair(q):
        return copy(pair_out.at[q], pair_in.at[q], pair_s.at[q], pair_r.at[q], sibling, z)

    for q in range(quarter):
        pair_out[q] = (dot(whole_t[(1 - core) * quarter + q], dh[...]) * scale).astype(BF16)
        pair(q).start()
    for q in range(quarter):
        gown[q] = dot(whole_t[core * quarter + q], dh[...]) * scale
    per = chips // quarter
    for q in range(quarter):
        pair(q).wait_recv()
        both = gown[q] + pair_in[q].astype(F32)
        rs_out[q * per:(q + 1) * per] = both.astype(BF16).reshape(per, width // per, width)

    for q in range(quarter):
        sent.append(functools.partial(lambda q: pair(q).wait_send(), q))

    def chip_at(i):
        return lax.rem(chip + i, chips)

    def rs(i):
        p = chip_at(i)
        return copy(rs_out.at[p], rs_in.at[chip], rs_s.at[p], rs_r.at[chip], p * 2 + core, z)

    def rs_wait(i):
        p = chip_at(i)
        copy(rs_out.at[p], rs_in.at[p], rs_s.at[p], rs_r.at[p], p * 2 + core, z).wait_recv()

    loop(1, chips, lambda i: rs(i).start())
    rs_in[chip] = rs_out[chip]
    loop(1, chips, rs_wait)
    sent.append(lambda: loop(1, chips, lambda i: rs(i).wait_send()))
    shard = rs_in[0].astype(F32)
    for p in range(1, chips):
        shard = shard + rs_in[p].astype(F32)
    gfull[core, chip] = shard.astype(BF16)
    energy = jnp.sum(jnp.sum(shard * shard, axis=1, keepdims=True), axis=0, keepdims=True)
    ez_out[...] = jnp.broadcast_to(energy, (8, 128))

    def ezc(i):
        zz = lax.rem(z + i, nz)
        return copy(ez_out, ez.at[z], ez_s.at[zz], ez_r.at[z], me, zz)

    def ezc_wait(i):
        zz = lax.rem(z + i, nz)
        copy(ez_out, ez.at[zz], ez_s.at[zz], ez_r.at[zz], me, zz).wait_recv()

    def ag(i):
        p = chip_at(i)
        return copy(gfull.at[core, chip], gfull.at[core, chip], ag_s.at[p], ag_r.at[chip], p * 2 + core, z)

    def ag_wait(i):
        p = lax.rem(chip - i + chips, chips)
        copy(gfull.at[core, p], gfull.at[core, p], ag_s.at[p], ag_r.at[p], p * 2 + core, z).wait_recv()
        return p

    def forward(p):
        return copy(gfull.at[core, p], gfull.at[core, p], fw_s.at[p], fw_r.at[p], sibling, z)

    def forward_wait(p):
        copy(gfull.at[1 - core, p], gfull.at[1 - core, p], fw_s.at[p], fw_r.at[p], sibling, z).wait_recv()

    loop(1, nz, lambda i: ezc(i).start())
    loop(1, chips, lambda i: ag(i).start())
    forward(chip).start()
    ez[z] = ez_out[...]
    loop(1, nz, ezc_wait)
    etot = ez[0]
    for i in range(1, nz):
        etot = etot + ez[i]
    row = iota((8, 128), 0)
    sent.append(lambda: loop(1, nz, lambda i: ezc(i).wait_send()))
    sent.append(lambda: loop(1, chips, lambda i: ag(i).wait_send()))
    sent.append(lambda: loop(0, chips, lambda p: forward(p).wait_send()))
    tile = jnp.where(row == 0, etot, jnp.where(row == 1, num, jnp.where(row == 2, den, over)))

    def dtc(i):
        d = nxt(i)
        return copy(dt_out, dt.at[me], dt_s.at[d], dt_r.at[me], d, z)

    def dtc_wait(i):
        h = prv(i)
        copy(dt_out, dt.at[h], dt_s.at[h], dt_r.at[h], h, z).wait_recv()

    dt_out[...] = tile
    loop(1, nd, lambda i: dtc(i).start())
    dt[me] = tile
    sent.append(lambda: loop(1, nd, lambda i: dtc(i).wait_send()))

    def ag_pass(i):
        p = ag_wait(i)
        forward(p).start()

    loop(1, chips, ag_pass)
    loop(1, nd, dtc_wait)
    total = dt[0]
    for i in range(1, nd):
        total = total + dt[i]
    entries = float(full_rows) * float(full_rows)
    factor = 0.5 * lax.rsqrt(total[0:1, 0:1] / entries + 1e-06)
    loss = total[1:2, :] / total[2:3, :]
    stat[...] = jnp.where(row == 0, loss, total[3:4, :])

    blk_rows = width // per

    def finish(h, p):
        r = pl.ds(pl.multiple_of((h * chips + p) * blk_rows, blk_rows), blk_rows)
        out[r, :] = (proj[r, :].astype(F32) - gfull[h, p].astype(F32) * factor).astype(BF16)

    loop(0, chips, lambda p: finish(core, p))

    def finish_far(p):
        forward_wait(p)
        finish(1 - core, p)

    loop(0, chips, finish_far)

    for wait in sent:
        wait()


def fast_step(nd, nz, feats, parent, counts, accepted, cand_ids, target_probs, gain, embed, proj):
    nodes, width = feats.shape
    full_rows = proj.shape[0]
    share = nodes // nd
    vocab = embed.shape[0]
    slots = nodes // 2
    chips = nd // 2
    quarter = nz // 2
    per = chips // quarter
    vm = pltpu.VMEM
    scratch = [
        vm((2, -(-vocab // 256) * 256, width), BF16),
        vm((nodes, nodes), BF16),
        vm((nodes, 128), BF16),
        vm((nd, share, 128), BF16),
        vm((nd, share, 128), BF16),
        vm((nd, share, width), BF16),
        vm((nd, share, width), BF16),
        vm((slots, nodes), BF16),
        vm((128, slots), F32),
        vm((chips, 8, CAPL), F32),
        vm((chips, 8, CAPL), F32),
        vm((chips, CAP, width), BF16),
        vm((chips, CAP, width), BF16),
        vm((nz, slots, width), BF16),
        vm((nz, width, slots), BF16),
        vm((slots, width), F32),
        vm((slots, width), BF16),
        vm((chips // GROUP, GROUP * CAP, slots), BF16),
        vm((chips // GROUP, slots, GROUP * CAPL), BF16),
        vm((GROUP * CAPL, 128), BF16),
        vm((chips // GROUP, GROUP * CAP, 128), BF16),
        vm((slots, 128), F32),
        vm((16, slots), F32),
        vm((nz, 16, slots), F32),
        vm((GROUP * CAPL, width), BF16),
        vm((slots, width), F32),
        vm((slots, width), BF16),
        vm((quarter, width, width), BF16),
        vm((quarter, width, width), BF16),
        vm((quarter, width, width), F32),
        vm((chips, width // per, width), BF16),
        vm((chips, width // per, width), BF16),
        vm((2, chips, width // per, width), BF16),
        vm((8, 128), F32),
        vm((nz, 8, 128), F32),
        vm((8, 128), F32),
        vm((nd, 8, 128), F32),
    ]
    dma = pltpu.SemaphoreType.DMA
    for count in (
        2, 2, nd, nd, nd, nd, chips, chips, chips, chips,
        nz, nz, nz, nz, nz, nz, quarter, quarter,
        chips, chips, chips, chips, chips, chips, nz, nz, nd, nd,
    ):
        scratch.append(dma((count,)))
    in_vmem = pl.BlockSpec(memory_space=pltpu.VMEM)
    out, stat = pl.pallas_call(
        functools.partial(step_kernel, nd, nz, full_rows),
        out_shape=(
            jax.ShapeDtypeStruct(proj.shape, BF16),
            jax.ShapeDtypeStruct((8, 128), F32),
        ),
        in_specs=[pl.BlockSpec(memory_space=pltpu.SMEM)] + [in_vmem] * 8,
        out_specs=(in_vmem, in_vmem),
        scratch_shapes=scratch,
        compiler_params=pltpu.CompilerParams(
            collective_id=0, has_side_effects=True, vmem_limit_bytes=60 * 1024 * 1024
        ),
        name="step",
    )(
        counts, cand_ids.T, target_probs.T, parent.reshape(8, nodes // 8), accepted.reshape(8, nodes // 8),
        feats, gain.reshape(1, width), embed, proj,
    )
    return out, stat


def every(x, axis):
    n = lax.axis_size(axis)
    return lax.all_to_all(jnp.broadcast_to(x[None], (n,) + x.shape), axis, 0, 0, tiled=True)


def total(x, axis):
    return jnp.sum(every(jnp.atleast_1d(x), axis), axis=0).reshape(x.shape)


def wide_step(feats, parent, counts, accepted, cand_ids, target_probs, gain, embed, proj):
    node_rows, width_part = feats.shape
    full_width = proj.shape[0]
    group = lax.axis_index("dp")
    groups = lax.axis_size("dp")
    shard_rows = embed.shape[0]
    cand_count = cand_ids.shape[1]
    scale_in = 1.0 / jnp.sqrt(jnp.float32(full_width))
    gain_f = gain.astype(jnp.float32)
    flat_ids = cand_ids.reshape(-1)
    requests = flat_ids.shape[0]
    capacity = 3 * requests // (2 * groups)
    owners = flat_ids // shard_rows
    local_ids = flat_ids - owners * shard_rows
    member = owners[:, None] == jnp.arange(groups, dtype=jnp.int32)[None, :]
    per_owner = jnp.sum(member.astype(jnp.int32), axis=0)
    starts = jnp.cumsum(per_owner) - per_owner
    my_start = jnp.sum(jnp.where(member, starts[None, :], 0), axis=1)
    order = jnp.argsort(owners, stable=True)
    ranks = jnp.arange(requests, dtype=jnp.int32) - my_start[order]
    slots = owners[order] * capacity + ranks
    outgoing = jnp.zeros((groups * capacity,), jnp.int32).at[slots].set(local_ids[order])
    placed = jnp.zeros((requests,), jnp.int32).at[order].set(slots)
    mixed = (feats.astype(jnp.float32) + feats[parent].astype(jnp.float32)).astype(jnp.bfloat16)
    piece = every(mixed, "mp").transpose(1, 0, 2).reshape(node_rows, full_width)
    partial_value = jnp.dot(piece, proj, preferred_element_type=jnp.float32)
    whole = piece
    partial_value, whole = (partial_value, whole)
    hidden = partial_value * scale_in
    squares = total(jnp.sum(hidden * hidden, axis=1), "mp")
    recip = lax.rsqrt(squares / full_width + 1e-05)
    normed = (hidden * recip[:, None] * gain_f).astype(jnp.bfloat16)
    found = embed[
        lax.all_to_all(
            outgoing.reshape(groups, capacity), "dp", split_axis=0, concat_axis=0, tiled=True
        )
    ]
    fetched = lax.all_to_all(found, "dp", split_axis=0, concat_axis=0, tiled=True)
    cand_rows = fetched.reshape(groups * capacity, width_part)[placed].reshape(
        node_rows, cand_count, width_part
    )
    part_scores = jnp.einsum("nkd,nd->nk", cand_rows, normed, preferred_element_type=jnp.float32)
    scores = total(part_scores, "mp")
    logp = scores - jnp.log(jnp.sum(jnp.exp(scores), axis=1, keepdims=True))
    prob = jnp.exp(logp)
    probs = target_probs.astype(jnp.float32)
    target = probs / jnp.sum(probs, axis=1, keepdims=True)
    kl_node = jnp.sum(target * (jnp.log(target) - logp), axis=1)
    live_count = lax.dynamic_index_in_dim(counts, group, 0, keepdims=False)
    live = jnp.arange(node_rows, dtype=jnp.int32) < live_count
    weight = jnp.where(live, 1 + accepted, 0).astype(jnp.float32)
    num, den = total(jnp.stack([jnp.sum(weight * kl_node), jnp.sum(weight)]), "dp")
    grad_scores = weight[:, None] * (prob - target)
    dnormed = jnp.einsum("nk,nkd->nd", grad_scores, cand_rows, preferred_element_type=jnp.float32)
    inner = total(jnp.sum(dnormed * gain_f * hidden, axis=1), "mp")
    dhidden = (
        recip[:, None] * gain_f * dnormed - hidden * (recip**3 * inner / full_width)[:, None]
    ).astype(jnp.bfloat16)
    grad_part = (
        lax.dot_general(
            whole, dhidden, (((0,), (0,)), ((), ())), preferred_element_type=jnp.float32
        )
        * scale_in
    )
    shares = lax.all_to_all(grad_part.reshape(groups, -1, width_part), "dp", 0, 0, tiled=True)
    grad = every(jnp.sum(shares, axis=0), "dp").reshape(full_width, width_part)
    energy = total(jnp.sum(grad * grad), "mp")
    factor = lax.rsqrt(energy / (full_width * full_width) + 1e-06)
    new_proj = (proj.astype(jnp.float32) - 0.5 * grad * factor).astype(jnp.bfloat16)
    return (new_proj, num / den)


def solution(mesh):
    nd = mesh.shape["dp"]
    nz = mesh.shape["mp"]

    def per_device(*args):
        out, stat = fast_step(nd, nz, *args)
        return lax.cond(
            stat[1, 0] > 0.0,
            lambda: wide_step(*args),
            lambda: (out, stat[0, 0]),
        )

    placed = (
        P("dp", "mp"),
        P("dp"),
        P(),
        P("dp"),
        P("dp", None),
        P("dp", None),
        P("mp"),
        P("dp", "mp"),
        P(None, "mp"),
    )
    return jax.shard_map(
        per_device, mesh=mesh, in_specs=placed, out_specs=(P(None, "mp"), P()), check_vma=False
    )
```

profile of v0, /device:TPU:1, one launch (start us, length us, event | category | flops | bytes accessed | tf_op | source)
XLA Modules:
  0.0 122.6 jit_solution(1919854951076628528)
XLA Ops:
  0.6 1.2 reshape.199.gain
  1.9 118.1 %step.1 = (bf16[2048,256]{1,0:T(8,128)(2,1)S(1)}, f32[8,128]{1,0:T(8,128)S(1)}) custom-call(s32[32]{0:T(128)} %counts.1, s32[8,1024]{1,0:T(8,128)} %bitcast.40, bf16[8,1024]{1,0:T(8,128)(2,1)} %bitcast.38, s32[8,128]{1,0:T(8,128)} %bitcast.44, s32[8,128]{1,0:T(8,128)} %bitcast.43, bf16[1024,256]{1,0:T(8,128)(2,1)} %feats.1, bf16[1,256]{1,0:T(2,128)(2,1)} %reshape.199.gain, ...), custom_call_target="tpu_custom_call" | custom-call | tf_op jit(solution)/shard_map/step/pallas_call | solution.py:643
  119.9 0.5 slice.6
  121.1 0.5 conditional.1
  121.1 0.5 slice.4
  121.6 1.0 copy.52
where the time goes:
time: 123 us
  Pallas kernels  118 us (96%)
  local copies, waits for them, and re-layouts  3.22 us (3%)
  between operations  1.29 us (1%)
    pallas_call x1, Pallas kernels, fast_step(): pl.pallas_call(functools.partial(step_kernel, nd, nz, full_rows), out_sha...  118 us

commit v1 on v0

v1 whole, which is shorter than its diff:
```python
import functools
import jax
import jax.numpy as jnp
from jax import lax
from jax.experimental import pallas as pl
from jax.experimental.pallas import tpu as pltpu
from jax.sharding import PartitionSpec as P

MESH = pl.DeviceIdType.MESH
F32 = jnp.float32
BF16 = jnp.bfloat16
I32 = jnp.int32

GROUP = 4
MIXLATE = 1
CAP = 352
CAPL = 384
HALF = 224


def dot(a, b):
    return jnp.dot(a, b, preferred_element_type=F32)


def dot_nt(a, b):
    return lax.dot_general(a, b, (((1,), (1,)), ((), ())), preferred_element_type=F32)


def one_hot(hit):
    return jnp.where(hit, 1.0, 0.0).astype(BF16)


def iota(shape, axis):
    return lax.broadcasted_iota(I32, shape, axis)


def step_kernel(
    nd, nz, full_rows,
    counts, ids, odds, parent, accepted, gain2, feats_in, embed_in, proj_in,
    out, loss_out, flag_out,
    feats, embed, proj, in_s, emb, perm, meta, mixat, metap, metar, mixp, mixr, live, metat,
    lists, sendid, idr, rows_out, rows_in, whole, whole_t, hidden, ng,
    pick_t, ksel_t, asked, sct, zsend, zr, dh,
    pair_out, pair_in, gown, rs_out, rs_in, gfull, sb_out, sb, ez_out, ez, dt_out, dt,
    emb_s, emb_r, meta_s, meta_r, mix_s, mix_r, id_s, id_r, row_s, row_r,
    zr_s, zr_r, zl_s, zl_r, zx_s, zx_r, pair_s, pair_r,
    rs_s, rs_r, ag_s, ag_r, fw_s, fw_r, sb_s, sb_r, ez_s, ez_r, dt_s, dt_r,
):
    me = lax.axis_index("dp")
    z = lax.axis_index("mp")
    nodes = feats.shape[0]
    width = feats.shape[1]
    slots = live.shape[1]
    share = nodes // nd
    core = lax.rem(me, 2)
    chip = lax.div(me, 2)
    chips = nd // 2
    sibling = me + 1 - 2 * core
    vocab = embed.shape[0]

    sent = []

    fetch = [
        pltpu.make_async_copy(src, dst, in_s.at[i])
        for i, (src, dst) in enumerate(((feats_in, feats), (embed_in, embed), (proj_in, proj)))
    ]
    for f in fetch:
        f.start()

    def copy(src, dst, ss, rs, d, zz):
        return pltpu.make_async_remote_copy(
            src_ref=src, dst_ref=dst, send_sem=ss, recv_sem=rs,
            device_id=(d, zz), device_id_type=MESH,
        )

    def nxt(i):
        return lax.rem(me + i, nd)

    def prv(i):
        return lax.rem(me - i + nd, nd)

    def loop(lo, hi, body):
        def wrapped(i, carry):
            body(i)
            return carry
        lax.fori_loop(lo, hi, wrapped, 0)

    side = int(chips ** 0.5)
    chip_x = lax.rem(chip, side)
    chip_y = lax.div(chip, side)

    def offset(i):
        dx = lax.rem(i, side)
        dy = lax.rem(lax.div(i, side) + i, side)
        return dx + core * (dy - dx), dy + core * (dx - dy)

    def to_chip(i):
        dx, dy = offset(i)
        return lax.rem(chip_y + dy, side) * side + lax.rem(chip_x + dx, side)

    def from_chip(i):
        dx, dy = offset(i)
        return lax.rem(chip_y - dy + side, side) * side + lax.rem(chip_x - dx + side, side)

    def chip_copy(src, dst, ss, rs, p):
        return copy(src.at[p], dst.at[chip], ss.at[p], rs.at[chip], p * 2 + core, z)

    def chip_wait(src, dst, ss, rs, p):
        copy(src.at[p], dst.at[p], ss.at[p], rs.at[p], p * 2 + core, z).wait_recv()

    def chip_sent_all(src, dst, ss, rs):
        loop(1, chips, lambda i: chip_copy(src, dst, ss, rs, to_chip(i)).wait_send())

    def dp_copy(src, dst, ss, rs, d):
        return copy(src.at[d], dst.at[me], ss.at[d], rs.at[me], d, z)

    def dp_wait(src, dst, ss, rs, h):
        copy(src.at[h], dst.at[h], ss.at[h], rs.at[h], h, z).wait_recv()

    def each_device(act):
        act(sibling)

        def both(i):
            act(to_chip(i) * 2 + core)
            act(to_chip(i) * 2 + 1 - core)

        loop(1, chips, both)

    def each_source(act):
        act(sibling)

        def both(i):
            act(from_chip(i) * 2 + core)
            act(from_chip(i) * 2 + 1 - core)

        loop(1, chips, both)

    def dp_send_all(src, dst, ss, rs):
        each_device(lambda d: dp_copy(src, dst, ss, rs, d).start())
        sent.append(lambda: dp_sent_all(src, dst, ss, rs))

    def dp_wait_all(src, dst, ss, rs):
        each_source(lambda h: dp_wait(src, dst, ss, rs, h))

    def dp_sent_all(src, dst, ss, rs):
        each_device(lambda d: dp_copy(src, dst, ss, rs, d).wait_send())

    barrier = pltpu.get_barrier_semaphore()
    loop(1, nd, lambda i: pl.semaphore_signal(barrier, inc=1, device_id=(nxt(i), z), device_id_type=MESH))
    loop(1, nz, lambda i: pl.semaphore_signal(barrier, inc=1, device_id=(me, lax.rem(z + i, nz)), device_id_type=MESH))

    pair_rows = share // 2
    node_lane = iota((1, nodes), 1)
    src_lane = iota((1, slots), 1)
    lane_h = lax.div(src_lane, pair_rows)
    lane_j = 2 * (src_lane - lane_h * pair_rows)

    def deal(h, state):
        off, mine, into0, into1 = state
        count = counts[h]
        first = (me - off) & (nd - 1)
        base = (off + first) // nd
        row0 = jnp.where(lane_j * nd + first < count, base + lane_j, -1)
        row1 = jnp.where((lane_j + 1) * nd + first < count, base + lane_j + 1, -1)
        here = lane_h == h
        return (
            off + count, jnp.where(h == me, off, mine),
            jnp.where(here, row0, into0), jnp.where(here, row1, into1),
        )

    none = jnp.full((1, slots), -1, I32)
    _, mine, into0, into1 = lax.fori_loop(0, nd, deal, (jnp.int32(0), jnp.int32(0), none, none))
    place_j = lax.div(node_lane, nd)
    dealt = (
        ((node_lane + mine) & (nd - 1)) * share
        + (place_j & 1) * pair_rows + lax.div(place_j, 2)
    )
    gain = jnp.concatenate([gain2[0:1, :], gain2[1:2, :]], axis=1).astype(F32)

    def in_row(ref):
        return jnp.concatenate([ref[r:r + 1, :] for r in range(ref.shape[0])], axis=1)

    idf = ids[...].astype(F32)
    own_f = jnp.floor((idf + 0.5) * (1.0 / float(vocab)))
    at_f = idf - own_f * float(vocab)
    hi_f = jnp.floor(at_f * (1.0 / 256.0))
    par = in_row(parent)
    extra = jnp.concatenate(
        [
            in_row(accepted).astype(F32),
            (par // 32).astype(F32),
            (par % 32).astype(F32),
            jnp.zeros((5, nodes), F32),
        ],
        axis=0,
    )
    table = jnp.concatenate(
        [own_f, hi_f + 1.0, at_f - 256.0 * hi_f, odds[...].astype(F32), extra, jnp.zeros((88, nodes), F32)],
        axis=0,
    )
    meta[...] = table.T.astype(BF16)

    step = 128

    def perm_block(b):
        rows = pl.ds(b * step, step)
        e = one_hot(iota((step, nodes), 0) + b * step == dealt)
        perm[rows, :] = e
        m = dot(e, meta[...])
        mixat[rows, :] = m
        m = m.astype(BF16).reshape(step // share, 2, pair_rows, 128)
        metap[pl.ds(b * (step // share), step // share)] = jnp.concatenate(
            [m[:, 0, :, 0:64], m[:, 1, :, 0:64]], axis=-1
        )

    loop(0, nodes // step, perm_block)

    fetch[1].wait()
    block = emb.shape[1]
    even = vocab // 32 * 32
    emb[core, 0:even, :] = embed[0:even, :]
    emb[core, even:block, :] = jnp.concatenate(
        [embed[even:vocab, :].astype(F32), jnp.zeros((block - vocab, width), F32)], axis=0
    ).astype(BF16)
    pl.semaphore_wait(barrier, nd - 1 + nz - 1)

    def emb_copy(c):
        return copy(emb.at[c], emb.at[c], emb_s.at[c], emb_r.at[c], sibling, z)

    emb_copy(core).start()
    sent.append(lambda: emb_copy(core).wait_send())
    dp_send_all(metap, metar, meta_s, meta_r)
    metar[me] = metap[me]

    def mixp_block(b):
        rows = pl.ds(b * step, step)
        at = mixat[rows, 33:34] * 32.0 + mixat[rows, 34:35]
        p = one_hot(iota((step, nodes), 1) == at.astype(I32))
        mixp[pl.ds(b * (step // share), step // share)] = (
            dot(perm[rows, :] + p, feats[...])
            .astype(BF16)
            .reshape(step // share, share, width)
        )

    fetch[0].wait()
    loop(0, nodes // step, mixp_block)
    if not MIXLATE:
        dp_send_all(mixp, mixr, mix_s, mix_r)
    mixr[me] = mixp[me]

    def live_block(b):
        at = iota((step, slots), 0) + b * step
        live[0, pl.ds(b * step, step), :] = one_hot(at == into0)
        live[1, pl.ds(b * step, step), :] = one_hot(at == into1)

    loop(0, slots // step, live_block)

    dp_wait_all(metap, metar, meta_s, meta_r)
    for b in range(slots // step):
        rows = slice(b * step, (b + 1) * step)
        got = metar[...].reshape(slots, metar.shape[2])
        part = dot(live[0, rows, :], got)[:, 0:64] + dot(live[1, rows, :], got)[:, 64:128]
        metat[:, rows] = part.T

    owner = metat[0:8, :].astype(I32)
    upper = one_hot(iota((slots, slots), 0) < iota((slots, slots), 1))
    own_iota = iota((nd, slots), 0)
    member = jnp.concatenate(
        [jnp.where(own_iota == owner[k:k + 1, :], 1.0, 0.0) for k in range(8)], axis=0
    )
    before = dot(member.astype(BF16), upper)
    carry = jnp.zeros((nd, 1), F32)
    found = jnp.zeros((chips * 8, CAPL), F32)
    asks = jnp.zeros((chips, 1), F32)
    at_chip = owner // 2
    odd_core = owner - 2 * at_chip
    chip_iota = iota((chips, slots), 0)
    node_row = iota((1, slots), 1)
    for k in range(8):
        mk = member[k * nd:(k + 1) * nd, :]
        rank = jnp.sum(mk * (before[k * nd:(k + 1) * nd, :] + carry), axis=0, keepdims=True)
        carry = carry + jnp.sum(mk, axis=1, keepdims=True)
        odd_k = odd_core[k:k + 1, :].astype(F32)
        place = rank + odd_k * (float(CAP - 1) - 2.0 * rank)
        asks = asks + jnp.sum(jnp.where(chip_iota == at_chip[k:k + 1, :], 1.0, 0.0), axis=1, keepdims=True)
        fields = jnp.concatenate(
            [
                metat[8 + k:9 + k, :] + float(block // 256) * odd_k,
                metat[16 + k:17 + k, :],
                (node_row // 2).astype(F32),
                ((node_row % 2) * 8 + (k + 1)).astype(F32),
                jnp.zeros((4, slots), F32),
            ],
            axis=0,
        )
        here = iota((chips, 8, slots), 0) == at_chip[k:k + 1, :][None]
        f = jnp.where(here, fields[None], 0.0).reshape(chips * 8, slots).astype(BF16)
        at = one_hot(iota((CAPL, slots), 0) == place.astype(I32))
        found = found + dot_nt(f, at)
    found = found.reshape(chips, 8, CAPL)
    lists[...] = found
    tiles = CAPL // 128
    sendid[...] = jnp.concatenate(
        [found[:, f:f + 1, t * 128:(t + 1) * 128] for f in range(2) for t in range(tiles)]
        + [jnp.zeros((chips, 8 - 2 * tiles, 128), F32)],
        axis=1,
    )
    over = jnp.maximum(
        jnp.max(jnp.where(carry > float(HALF), 1.0, 0.0), axis=0, keepdims=True),
        jnp.max(jnp.where(asks > float(CAP), 1.0, 0.0), axis=0, keepdims=True),
    )
    loop(1, chips, lambda i: chip_copy(sendid, idr, id_s, id_r, to_chip(i)).start())
    sent.append(lambda: chip_sent_all(sendid, idr, id_s, id_r))
    idr[chip] = sendid[chip]
    if MIXLATE:
        dp_send_all(mixp, mixr, mix_s, mix_r)

    def owner_at(j, q):
        return from_chip(j * GROUP + q + 1)

    groups = chips // GROUP

    def pick_group(j):
        for q in range(GROUP):
            a = lists[owner_at(j, q), 2:3, :]
            b = lists[owner_at(j, q), 3:4, :]
            odd = jnp.where(b - 1.0 >= 8.0, 1.0, 0.0)
            node = jnp.where(b > 0.0, 2.0 * a + odd, -1.0).astype(I32)
            k = jnp.where(b > 0.0, b - 1.0 - 8.0 * odd, -1.0).astype(I32)
            pick_t[j, :, q * CAPL:(q + 1) * CAPL] = one_hot(iota((slots, CAPL), 0) == node)
            ksel_t[j, :, q * CAPL:(q + 1) * CAPL] = jnp.where(iota((8, CAPL), 0) == k, 1.0, 0.0)

    def ask_group(j):
        got = lax.dot_general(pick_t[j], ng[...], (((0,), (0,)), ((), ())), preferred_element_type=F32)
        asked[j] = got.astype(BF16)

    def score(j, arrivals):
        for q in range(arrivals):
            wait_row(j * GROUP + q + 1)
        got = rows_in[j * GROUP:(j + 1) * GROUP].reshape(GROUP * CAPL, width).astype(F32)
        s = jnp.sum(got * asked[j].astype(F32), axis=1, keepdims=True)
        s = jnp.broadcast_to(s, (GROUP * CAPL, 128)).T[0:8, :]
        s_hi = s.astype(BF16).astype(F32)
        by_k = jnp.concatenate([s_hi * ksel_t[j], (s - s_hi) * ksel_t[j]], axis=0).astype(BF16)
        return dot_nt(by_k, pick_t[j])

    def mix_in():
        dp_wait_all(mixp, mixr, mix_s, mix_r)
        for b in range(slots // step):
            rows = slice(b * step, (b + 1) * step)
            part = dot(live[0, rows, :], mixr[:, 0:pair_rows, :].reshape(slots, width)) + dot(
                live[1, rows, :], mixr[:, pair_rows:share, :].reshape(slots, width)
            )
            whole[z, rows, :] = part.astype(BF16)

    if not MIXLATE:
        mix_in()
    zright = lax.rem(z + 1, nz)
    zleft = lax.rem(z + nz - 1, nz)

    def ring_part(s, first):
        if s + 1 < nz // 2:
            return pl.ds(0, slots)
        return pl.ds(first * (slots // 2), slots // 2)

    def ring_copy(s, b, side_r):
        rows = ring_part(s, 0 if side_r else 1)
        ss, rs = (zr_s, zr_r) if side_r else (zl_s, zl_r)
        return copy(
            whole.at[b, rows], whole.at[b, rows], ss.at[s], rs.at[s], me, zright if side_r else zleft
        )

    def ring_right(s):
        return ring_copy(s, lax.rem(z - s + nz, nz), True)

    def ring_left(s):
        return ring_copy(s, lax.rem(z + s, nz), False)

    def got_right(s):
        b = lax.rem(z - s - 1 + nz, nz)
        ring_copy(s, b, True).wait_recv()
        return b

    def got_left(s):
        b = lax.rem(z + s + 1, nz)
        ring_copy(s, b, False).wait_recv()
        return b

    hops = nz // 2
    if not MIXLATE:
        ring_right(0).start()
        ring_left(0).start()
    for j in range(groups):
        pick_group(j)
    scale = 1.0 / (float(full_rows) ** 0.5)

    def use_block(b, first=False):
        blk = whole[b]
        whole_t[b] = blk.T
        h = dot(blk, proj[pl.ds(pl.multiple_of(b * width, width), width), :])
        if first:
            hidden[...] = h
        else:
            hidden[...] += h

    chunk = 256

    low = CAP - HALF

    def serve(h):
        cols = idr[h].T
        hi = jnp.concatenate([cols[:, t:t + 1] for t in range(tiles)], axis=0)[:CAP]
        lo = jnp.concatenate([cols[:, tiles + t:tiles + t + 1] for t in range(tiles)], axis=0)[:CAP]
        hi = jnp.broadcast_to(hi, (CAP, chunk)).astype(BF16)
        lo = one_hot(iota((CAP, chunk), 1) == lo.astype(I32))
        halves = []
        for c in range(2):
            first = c * low
            parts = [
                jnp.where(
                    hi[first:first + HALF, :] == jnp.bfloat16(c * (block // chunk) + i + 1),
                    lo[first:first + HALF, :],
                    jnp.bfloat16(0),
                )
                for i in range(block // chunk)
            ]
            halves.append(dot(jnp.concatenate(parts, axis=1), emb[c]))
        front, rear = halves
        rows_out[h, 0:low, :] = front[0:low, :].astype(BF16)
        rows_out[h, low:HALF, :] = (front[low:, :] + rear[:HALF - low, :]).astype(BF16)
        rows_out[h, HALF:CAP, :] = rear[HALF - low:, :].astype(BF16)

    def row_copy(i):
        p = to_chip(i)
        used = pl.ds(0, CAP)
        return copy(
            rows_out.at[p, used], rows_in.at[i - 1, used], row_s.at[p], row_r.at[i - 1], p * 2 + core, z
        )

    def wait_row(i):
        p = from_chip(i)
        used = pl.ds(0, CAP)
        copy(
            rows_out.at[p, used], rows_in.at[i - 1, used], row_s.at[p], row_r.at[i - 1], p * 2 + core, z
        ).wait_recv()

    def serve_far(i):
        h = to_chip(i)
        chip_wait(sendid, idr, id_s, id_r, h)
        serve(h)
        row_copy(i).start()

    emb_copy(1 - core).wait_recv()
    fetch[2].wait()
    done = 1
    if MIXLATE:
        loop(done, 4, serve_far)
        done = 4
        mix_in()
        ring_right(0).start()
        ring_left(0).start()
    use_block(z, True)
    for s in range(hops):
        upto = min(done + 5, chips)
        loop(done, upto, serve_far)
        done = upto
        if s + 2 == hops:
            loop(done, chips, serve_far)
            done = chips
            serve(chip)
        b = got_right(s)
        if s + 1 < hops:
            ring_right(s + 1).start()
            use_block(b)
        b = got_left(s)
        if s + 1 < hops:
            ring_left(s + 1).start()
        use_block(b)
    rows_in[chips - 1, 0:CAP, :] = rows_out[chip, 0:CAP, :]
    rows_in[:, CAP:CAPL, :] = jnp.zeros((chips, CAPL - CAP, width), BF16)
    sent.append(lambda: loop(1, chips, lambda i: row_copy(i).wait_send()))
    for s in range(hops):
        sent.append(functools.partial(lambda s: ring_right(s).wait_send(), s))
        sent.append(functools.partial(lambda s: ring_left(s).wait_send(), s))

    hid = hidden[...] * scale
    hidden[...] = hid
    square = jnp.sum(hid * hid, axis=1, keepdims=True)
    ng[...] = (hid * gain).astype(BF16)
    square = jnp.broadcast_to(square, (slots, 128)).T[0:1, :]
    for j in range(groups):
        ask_group(j)
    got = score(0, GROUP)
    for j in range(1, groups):
        got = got + score(j, GROUP - (j + 1) // groups)

    zsend[:, 0:slots] = got[0:8, :] + got[8:16, :]
    folds = slots // 128
    zsend[:, slots:slots + 128] = jnp.concatenate(
        [square[:, f * 128:(f + 1) * 128] for f in range(folds)] + [jnp.zeros((8 - folds, 128), F32)], axis=0
    )

    def zx(i):
        zz = lax.rem(z + i, nz)
        return copy(zsend, zr.at[z], zx_s.at[zz], zx_r.at[z], me, zz)

    def zx_wait(i):
        zz = lax.rem(z + i, nz)
        copy(zsend, zr.at[zz], zx_s.at[zz], zx_r.at[zz], me, zz).wait_recv()

    loop(1, nz, lambda i: zx(i).start())
    sent.append(lambda: loop(1, nz, lambda i: zx(i).wait_send()))
    zr[z] = zsend[...]
    loop(1, nz, zx_wait)
    tot = zr[0]
    for i in range(1, nz):
        tot = tot + zr[i]
    raw = tot[:, 0:slots]
    squares = jnp.concatenate([tot[f:f + 1, slots:slots + 128] for f in range(folds)], axis=1)
    recip = lax.rsqrt(squares / float(full_rows) + 1e-05)
    scores = raw * recip
    logp = scores - jnp.log(jnp.sum(jnp.exp(scores), axis=0, keepdims=True))
    prob = jnp.exp(logp)
    probs = metat[24:32, :]
    target = probs / jnp.sum(probs, axis=0, keepdims=True)
    kl = jnp.sum(target * (jnp.log(target) - logp), axis=0, keepdims=True)
    weight = 1.0 + metat[32:33, :]
    num = jnp.sum(weight * kl, axis=1, keepdims=True)
    den = jnp.sum(weight, axis=1, keepdims=True)
    gs = weight * (prob - target)
    inner = jnp.sum(gs * raw, axis=0, keepdims=True)
    back = recip * recip * recip * inner * (1.0 / float(full_rows))
    gs_hi = gs.astype(BF16).astype(F32)
    gs16 = jnp.concatenate([gs_hi, gs - gs_hi], axis=0).astype(BF16)
    coef = jnp.concatenate([recip, back, jnp.zeros((6, slots), F32)], axis=0).T

    for j in range(groups):
        g16 = dot(gs16, pick_t[j])
        g = jnp.sum((g16[0:8, :] + g16[8:16, :]) * ksel_t[j], axis=0, keepdims=True)
        scaled = pick_t[j] * g.astype(BF16)
        part = dot(scaled, rows_in[j * GROUP:(j + 1) * GROUP].reshape(GROUP * CAPL, width))
        dnormed = part if j == 0 else dnormed + part
    dh[...] = (coef[:, 0:1] * gain * dnormed - hidden[...] * coef[:, 1:2]).astype(BF16)

    quarter = nz // 2

    def pair(q):
        return copy(pair_out.at[q], pair_in.at[q], pair_s.at[q], pair_r.at[q], sibling, z)

    def turn(q):
        return lax.rem(chip_y + q, quarter)

    for q in range(quarter):
        pair_out[q] = (dot(whole_t[(1 - core) * quarter + turn(q)], dh[...]) * scale).astype(BF16)
        pair(q).start()
    for q in range(quarter):
        gown[q] = dot(whole_t[core * quarter + turn(q)], dh[...]) * scale
    per = chips // quarter

    def rs_copy(p):
        return chip_copy(rs_out, rs_in, rs_s, rs_r, p)

    for q in range(quarter):
        pair(q).wait_recv()
        both = gown[q] + pair_in[q].astype(F32)
        first = turn(q) * per
        rs_out[pl.ds(first, per)] = both.astype(BF16).reshape(per, width // per, width)
        for i in range(1 if q == 0 else 0, per):
            rs_copy(first + lax.rem(chip_x + i, per)).start()
    for q in range(quarter):
        sent.append(functools.partial(lambda q: pair(q).wait_send(), q))

    def chip_got(src, dst, ss, rs):
        loop(1, chips, lambda i: chip_wait(src, dst, ss, rs, from_chip(i)))

    sent.append(lambda: chip_sent_all(rs_out, rs_in, rs_s, rs_r))
    rs_in[chip] = rs_out[chip]
    chip_got(rs_out, rs_in, rs_s, rs_r)
    shard = rs_in[0].astype(F32)
    for p in range(1, chips):
        shard = shard + rs_in[p].astype(F32)
    gfull[core, chip] = shard.astype(BF16)
    energy = jnp.sum(jnp.sum(shard * shard, axis=1, keepdims=True), axis=0, keepdims=True)
    row = iota((8, 128), 0)
    tile = jnp.where(row == 0, energy, jnp.where(row == 1, num, jnp.where(row == 2, den, over)))

    sb_out[...] = tile
    both_cores = copy(sb_out, sb, sb_s.at[0], sb_r.at[0], sibling, z)
    both_cores.start()

    def ezc(i):
        zz = lax.rem(z + i, nz)
        return copy(ez_out, ez.at[z], ez_s.at[zz], ez_r.at[z], me, zz)

    def ezc_wait(i):
        zz = lax.rem(z + i, nz)
        copy(ez_out, ez.at[zz], ez_s.at[zz], ez_r.at[zz], me, zz).wait_recv()

    def ag(i):
        p = to_chip(i)
        return copy(gfull.at[core, chip], gfull.at[core, chip], ag_s.at[p], ag_r.at[chip], p * 2 + core, z)

    def ag_wait(i):
        p = from_chip(i)
        copy(gfull.at[core, p], gfull.at[core, p], ag_s.at[p], ag_r.at[p], p * 2 + core, z).wait_recv()
        return p

    def forward(p):
        return copy(gfull.at[core, p], gfull.at[core, p], fw_s.at[p], fw_r.at[p], sibling, z)

    def forward_wait(p):
        copy(gfull.at[1 - core, p], gfull.at[1 - core, p], fw_s.at[p], fw_r.at[p], sibling, z).wait_recv()

    sent.append(both_cores.wait_send)
    sent.append(lambda: loop(1, nz, lambda i: ezc(i).wait_send()))
    sent.append(lambda: loop(1, chips, lambda i: ag(i).wait_send()))
    sent.append(lambda: loop(0, chips, lambda p: forward(p).wait_send()))

    loop(1, chips, lambda i: ag(i).start())
    forward(chip).start()
    both_cores.wait_recv()
    tile = tile + sb[...]
    ez_out[...] = tile
    loop(1, nz, lambda i: ezc(i).start())
    ez[z] = tile
    loop(1, nz, ezc_wait)
    etot = ez[0]
    for i in range(1, nz):
        etot = etot + ez[i]
    tile = jnp.where(row == 0, etot, tile)
    dt_out[...] = tile

    def dtc(i):
        p = to_chip(i)
        return copy(dt_out, dt.at[chip], dt_s.at[p], dt_r.at[chip], p * 2 + core, z)

    def dtc_wait(i):
        p = from_chip(i)
        copy(dt_out, dt.at[p], dt_s.at[p], dt_r.at[p], p * 2 + core, z).wait_recv()

    loop(1, chips, lambda i: dtc(i).start())
    sent.append(lambda: loop(1, chips, lambda i: dtc(i).wait_send()))
    dt[chip] = tile

    def ag_pass(i):
        p = ag_wait(i)
        forward(p).start()

    loop(1, chips, ag_pass)
    loop(1, chips, dtc_wait)
    total = dt[0]
    for i in range(1, chips):
        total = total + dt[i]
    entries = float(full_rows) * float(full_rows)
    factor = 0.5 * lax.rsqrt(total[0:1, 0:1] / entries + 1e-06)
    loss_out[...] = total[1:2, 0:1] / total[2:3, 0:1]
    flag_out[...] = total[3:4, 0:1]

    blk_rows = width // per

    def finish(h, p):
        r = pl.ds(pl.multiple_of((h * chips + p) * blk_rows, blk_rows), blk_rows)
        out[r, :] = (proj[r, :].astype(F32) - gfull[h, p].astype(F32) * factor).astype(BF16)

    loop(0, chips, lambda p: finish(core, p))

    def finish_far(p):
        forward_wait(p)
        finish(1 - core, p)

    loop(0, chips, finish_far)

    for wait in sent:
        wait()


def fast_step(nd, nz, feats, parent, counts, accepted, cand_ids, target_probs, gain, embed, proj):
    nodes, width = feats.shape
    full_rows = proj.shape[0]
    share = nodes // nd
    vocab = embed.shape[0]
    slots = nodes // 2
    chips = nd // 2
    quarter = nz // 2
    per = chips // quarter
    vm = pltpu.VMEM
    scratch = [
        vm(feats.shape, BF16),
        vm(embed.shape, BF16),
        vm(proj.shape, BF16),
        pltpu.SemaphoreType.DMA((3,)),
        vm((2, -(-vocab // 256) * 256, width), BF16),
        vm((nodes, nodes), BF16),
        vm((nodes, 128), BF16),
        vm((nodes, 128), F32),
        vm((nd, share // 2, 128), BF16),
        vm((nd, share // 2, 128), BF16),
        vm((nd, share, width), BF16),
        vm((nd, share, width), BF16),
        vm((2, slots, slots), BF16),
        vm((64, slots), F32),
        vm((chips, 8, CAPL), F32),
        vm((chips, 8, 128), F32),
        vm((chips, 8, 128), F32),
        vm((chips, CAPL, width), BF16),
        vm((chips, CAPL, width), BF16),
        vm((nz, slots, width), BF16),
        vm((nz, width, slots), BF16),
        vm((slots, width), F32),
        vm((slots, width), BF16),
        vm((chips // GROUP, slots, GROUP * CAPL), BF16),
        vm((chips // GROUP, 8, GROUP * CAPL), F32),
        vm((chips // GROUP, GROUP * CAPL, width), BF16),
        vm((16, slots), F32),
        vm((8, slots + 128), F32),
        vm((nz, 8, slots + 128), F32),
        vm((slots, width), BF16),
        vm((quarter, width, width), BF16),
        vm((quarter, width, width), BF16),
        vm((quarter, width, width), F32),
        vm((chips, width // per, width), BF16),
        vm((chips, width // per, width), BF16),
        vm((2, chips, width // per, width), BF16),
        vm((8, 128), F32),
        vm((8, 128), F32),
        vm((8, 128), F32),
        vm((nz, 8, 128), F32),
        vm((8, 128), F32),
        vm((chips, 8, 128), F32),
    ]
    dma = pltpu.SemaphoreType.DMA
    for count in (
        2, 2, nd, nd, nd, nd, chips, chips, chips, chips,
        nz, nz, nz, nz, nz, nz, quarter, quarter,
        chips, chips, chips, chips, chips, chips, 1, 1, nz, nz, chips, chips,
    ):
        scratch.append(dma((count,)))
    in_vmem = pl.BlockSpec(memory_space=pltpu.VMEM)
    return pl.pallas_call(
        functools.partial(step_kernel, nd, nz, full_rows),
        out_shape=(
            jax.ShapeDtypeStruct(proj.shape, BF16),
            jax.ShapeDtypeStruct((1, 1), F32),
            jax.ShapeDtypeStruct((1, 1), F32),
        ),
        in_specs=[pl.BlockSpec(memory_space=pltpu.SMEM)] + [in_vmem] * 5 + [pl.BlockSpec(memory_space=pl.ANY)] * 3,
        out_specs=(in_vmem, in_vmem, in_vmem),
        scratch_shapes=scratch,
        compiler_params=pltpu.CompilerParams(
            collective_id=0, has_side_effects=True, vmem_limit_bytes=60 * 1024 * 1024
        ),
        name="step",
    )(
        counts, cand_ids.T, target_probs.T, parent.reshape(8, nodes // 8), accepted.reshape(8, nodes // 8),
        gain.reshape(2, width // 2), feats, embed, proj,
    )


def every(x, axis):
    n = lax.axis_size(axis)
    return lax.all_to_all(jnp.broadcast_to(x[None], (n,) + x.shape), axis, 0, 0, tiled=True)


def total(x, axis):
    return jnp.sum(every(jnp.atleast_1d(x), axis), axis=0).reshape(x.shape)


def wide_step(feats, parent, counts, accepted, cand_ids, target_probs, gain, embed, proj):
    node_rows, width_part = feats.shape
    full_width = proj.shape[0]
    group = lax.axis_index("dp")
    groups = lax.axis_size("dp")
    shard_rows = embed.shape[0]
    cand_count = cand_ids.shape[1]
    scale_in = 1.0 / jnp.sqrt(jnp.float32(full_width))
    gain_f = gain.astype(jnp.float32)
    flat_ids = cand_ids.reshape(-1)
    requests = flat_ids.shape[0]
    capacity = 3 * requests // (2 * groups)
    owners = flat_ids // shard_rows
    local_ids = flat_ids - owners * shard_rows
    member = owners[:, None] == jnp.arange(groups, dtype=jnp.int32)[None, :]
    per_owner = jnp.sum(member.astype(jnp.int32), axis=0)
    starts = jnp.cumsum(per_owner) - per_owner
    my_start = jnp.sum(jnp.where(member, starts[None, :], 0), axis=1)
    order = jnp.argsort(owners, stable=True)
    ranks = jnp.arange(requests, dtype=jnp.int32) - my_start[order]
    slots = owners[order] * capacity + ranks
    outgoing = jnp.zeros((groups * capacity,), jnp.int32).at[slots].set(local_ids[order])
    placed = jnp.zeros((requests,), jnp.int32).at[order].set(slots)
    mixed = (feats.astype(jnp.float32) + feats[parent].astype(jnp.float32)).astype(jnp.bfloat16)
    piece = every(mixed, "mp").transpose(1, 0, 2).reshape(node_rows, full_width)
    partial_value = jnp.dot(piece, proj, preferred_element_type=jnp.float32)
    whole = piece
    partial_value, whole = (partial_value, whole)
    hidden = partial_value * scale_in
    squares = total(jnp.sum(hidden * hidden, axis=1), "mp")
    recip = lax.rsqrt(squares / full_width + 1e-05)
    normed = (hidden * recip[:, None] * gain_f).astype(jnp.bfloat16)
    found = embed[
        lax.all_to_all(
            outgoing.reshape(groups, capacity), "dp", split_axis=0, concat_axis=0, tiled=True
        )
    ]
    fetched = lax.all_to_all(found, "dp", split_axis=0, concat_axis=0, tiled=True)
    cand_rows = fetched.reshape(groups * capacity, width_part)[placed].reshape(
        node_rows, cand_count, width_part
    )
    part_scores = jnp.einsum("nkd,nd->nk", cand_rows, normed, preferred_element_type=jnp.float32)
    scores = total(part_scores, "mp")
    logp = scores - jnp.log(jnp.sum(jnp.exp(scores), axis=1, keepdims=True))
    prob = jnp.exp(logp)
    probs = target_probs.astype(jnp.float32)
    target = probs / jnp.sum(probs, axis=1, keepdims=True)
    kl_node = jnp.sum(target * (jnp.log(target) - logp), axis=1)
    live_count = lax.dynamic_index_in_dim(counts, group, 0, keepdims=False)
    live = jnp.arange(node_rows, dtype=jnp.int32) < live_count
    weight = jnp.where(live, 1 + accepted, 0).astype(jnp.float32)
    num, den = total(jnp.stack([jnp.sum(weight * kl_node), jnp.sum(weight)]), "dp")
    grad_scores = weight[:, None] * (prob - target)
    dnormed = jnp.einsum("nk,nkd->nd", grad_scores, cand_rows, preferred_element_type=jnp.float32)
    inner = total(jnp.sum(dnormed * gain_f * hidden, axis=1), "mp")
    dhidden = (
        recip[:, None] * gain_f * dnormed - hidden * (recip**3 * inner / full_width)[:, None]
    ).astype(jnp.bfloat16)
    grad_part = (
        lax.dot_general(
            whole, dhidden, (((0,), (0,)), ((), ())), preferred_element_type=jnp.float32
        )
        * scale_in
    )
    shares = lax.all_to_all(grad_part.reshape(groups, -1, width_part), "dp", 0, 0, tiled=True)
    grad = every(jnp.sum(shares, axis=0), "dp").reshape(full_width, width_part)
    energy = total(jnp.sum(grad * grad), "mp")
    factor = lax.rsqrt(energy / (full_width * full_width) + 1e-06)
    new_proj = (proj.astype(jnp.float32) - 0.5 * grad * factor).astype(jnp.bfloat16)
    return (new_proj, num / den)


def solution(mesh):
    nd = mesh.shape["dp"]
    nz = mesh.shape["mp"]

    def per_device(*args):
        out, loss, flag = fast_step(nd, nz, *args)
        return lax.cond(
            flag[0, 0] > 0.0,
            lambda: wide_step(*args),
            lambda: (out, loss[0, 0]),
        )

    placed = (
        P("dp", "mp"),
        P("dp"),
        P(),
        P("dp"),
        P("dp", None),
        P("dp", None),
        P("mp"),
        P("dp", "mp"),
        P(None, "mp"),
    )
    return jax.shard_map(
        per_device, mesh=mesh, in_specs=placed, out_specs=(P(None, "mp"), P()), check_vma=False
    )
```

time: 123 us -> 108 us (0.88)
  Pallas kernels: 118 us -> 104 us
  local copies, waits for them, and re-layouts: 3.22 us -> 0.97 us
  between operations: 1.29 us -> 3.03 us
    pallas_call x1, Pallas kernels: 118 us -> 104 us  [fast_step(): pl.pallas_call(functools.partial(step_kernel, nd, nz, full_rows), out_sha...]
where the time goes in v1:
time: 108 us
  Pallas kernels  104 us (96%)
  between operations  3.03 us (3%)
    pallas_call x1, Pallas kernels, fast_step(): pl.pallas_call(functools.partial(step_kernel, nd, nz, full_rows), out_sha...  104 us

profile of v1, /device:TPU:1, one launch (start us, length us, event | category | flops | bytes accessed | tf_op | source)
XLA Modules:
  0.0 108.1 jit_solution(14018037565927174091)
XLA Ops:
  0.6 103.8 %step.1 = (bf16[2048,256]{1,0:T(8,128)(2,1)S(1)}, f32[1,1]{1,0:T(1,128)}, f32[1,1]{1,0:T(1,128)}) custom-call(s32[32]{0:T(128)} %counts.1, s32[8,1024]{1,0:T(8,128)} %bitcast.41, bf16[8,1024]{1,0:T(8,128)(2,1)} %bitcast.39, s32[8,128]{1,0:T(8,128)} %bitcast.45, s32[8,128]{1,0:T(8,128)} %bitcast.44, bf16[2,128]{1,0:T(2,128)(2,1)} %bitcast.47, ...), custom_call_target="tpu_custom_call" | custom-call | tf_op jit(solution)/shard_map/step/pallas_call | solution.py:739
  105.1 0.3 conditional.1
  105.4 1.0 copy.53

commit v2 on v1

--- a/solution.py
+++ b/solution.py
@@ -12,7 +12,8 @@
 I32 = jnp.int32
 
 GROUP = 4
-MIXLATE = 1
+MIXFIRST = 1
+CH = 1
 CAP = 352
 CAPL = 384
 HALF = 224
@@ -40,10 +41,10 @@
     out, loss_out, flag_out,
     feats, embed, proj, in_s, emb, perm, meta, mixat, metap, metar, mixp, mixr, live, metat,
     lists, sendid, idr, rows_out, rows_in, whole, whole_t, hidden, ng,
-    pick_t, ksel_t, asked, sct, zsend, zr, dh,
+    pick_t, ksel_t, asked, zq, zqr, zs, zsr, dh,
     pair_out, pair_in, gown, rs_out, rs_in, gfull, sb_out, sb, ez_out, ez, dt_out, dt,
     emb_s, emb_r, meta_s, meta_r, mix_s, mix_r, id_s, id_r, row_s, row_r,
-    zr_s, zr_r, zl_s, zl_r, zx_s, zx_r, pair_s, pair_r,
+    zr_s, zr_r, zl_s, zl_r, zx_s, zx_r, zq_s, zq_r, pair_s, pair_r,
     rs_s, rs_r, ag_s, ag_r, fw_s, fw_r, sb_s, sb_r, ez_s, ez_r, dt_s, dt_r,
 ):
     me = lax.axis_index("dp")
@@ -98,24 +99,19 @@
         dx, dy = offset(i)
         return lax.rem(chip_y + dy, side) * side + lax.rem(chip_x + dx, side)
 
-    def from_chip(i):
+    def from_chip(i, sibling_order=False):
         dx, dy = offset(i)
+        if sibling_order:
+            dx, dy = dy, dx
         return lax.rem(chip_y - dy + side, side) * side + lax.rem(chip_x - dx + side, side)
 
-    def chip_copy(src, dst, ss, rs, p):
-        return copy(src.at[p], dst.at[chip], ss.at[p], rs.at[chip], p * 2 + core, z)
-
-    def chip_wait(src, dst, ss, rs, p):
-        copy(src.at[p], dst.at[p], ss.at[p], rs.at[p], p * 2 + core, z).wait_recv()
-
-    def chip_sent_all(src, dst, ss, rs):
-        loop(1, chips, lambda i: chip_copy(src, dst, ss, rs, to_chip(i)).wait_send())
-
-    def dp_copy(src, dst, ss, rs, d):
-        return copy(src.at[d], dst.at[me], ss.at[d], rs.at[me], d, z)
-
-    def dp_wait(src, dst, ss, rs, h):
-        copy(src.at[h], dst.at[h], ss.at[h], rs.at[h], h, z).wait_recv()
+    others = chips - 1
+
+    def round_got(dst, rs):
+        copy(dst, dst, rs, rs, sibling, z).wait_recv()
+
+    def round_sent(src, ss):
+        copy(src, src, ss, ss, sibling, z).wait_send()
 
     def each_device(act):
         act(sibling)
@@ -126,24 +122,22 @@
 
         loop(1, chips, both)
 
-    def each_source(act):
-        act(sibling)
-
-        def both(i):
-            act(from_chip(i) * 2 + core)
-            act(from_chip(i) * 2 + 1 - core)
-
-        loop(1, chips, both)
-
-    def dp_send_all(src, dst, ss, rs):
-        each_device(lambda d: dp_copy(src, dst, ss, rs, d).start())
-        sent.append(lambda: dp_sent_all(src, dst, ss, rs))
-
-    def dp_wait_all(src, dst, ss, rs):
-        each_source(lambda h: dp_wait(src, dst, ss, rs, h))
-
-    def dp_sent_all(src, dst, ss, rs):
-        each_device(lambda d: dp_copy(src, dst, ss, rs, d).wait_send())
+    def z_round(src, dst, ss, rs):
+        def one(i):
+            copy(src, dst.at[z], ss, rs, me, lax.rem(z + i, nz)).start()
+
+        loop(1, nz, one)
+        sent.append(lambda: round_sent(dst.at[pl.ds(0, nz - 1)], ss))
+
+    def z_got(dst, rs):
+        round_got(dst.at[pl.ds(0, nz - 1)], rs)
+
+    def dp_round(src, dst, ss, rs):
+        each_device(lambda d: copy(src.at[d], dst.at[me], ss.at[0], rs.at[0], d, z).start())
+        sent.append(lambda: round_sent(src.at[pl.ds(0, nd - 1)], ss.at[0]))
+
+    def dp_got(dst, rs):
+        round_got(dst.at[pl.ds(0, nd - 1)], rs.at[0])
 
     barrier = pltpu.get_barrier_semaphore()
     loop(1, nd, lambda i: pl.semaphore_signal(barrier, inc=1, device_id=(nxt(i), z), device_id_type=MESH))
@@ -229,7 +223,7 @@
 
     emb_copy(core).start()
     sent.append(lambda: emb_copy(core).wait_send())
-    dp_send_all(metap, metar, meta_s, meta_r)
+    dp_round(metap, metar, meta_s, meta_r)
     metar[me] = metap[me]
 
     def mixp_block(b):
@@ -244,8 +238,8 @@
 
     fetch[0].wait()
     loop(0, nodes // step, mixp_block)
-    if not MIXLATE:
-        dp_send_all(mixp, mixr, mix_s, mix_r)
+    if MIXFIRST:
+        dp_round(mixp, mixr, mix_s, mix_r)
     mixr[me] = mixp[me]
 
     def live_block(b):
@@ -255,7 +249,7 @@
 
     loop(0, slots // step, live_block)
 
-    dp_wait_all(metap, metar, meta_s, meta_r)
+    dp_got(metar, meta_r)
     for b in range(slots // step):
         rows = slice(b * step, (b + 1) * step)
         got = metar[...].reshape(slots, metar.shape[2])
@@ -309,11 +303,16 @@
         jnp.max(jnp.where(carry > float(HALF), 1.0, 0.0), axis=0, keepdims=True),
         jnp.max(jnp.where(asks > float(CAP), 1.0, 0.0), axis=0, keepdims=True),
     )
-    loop(1, chips, lambda i: chip_copy(sendid, idr, id_s, id_r, to_chip(i)).start())
-    sent.append(lambda: chip_sent_all(sendid, idr, id_s, id_r))
+
+    def ask(i):
+        p = to_chip(i)
+        copy(sendid.at[p], idr.at[chip], id_s.at[0], id_r.at[chip], p * 2 + core, z).start()
+
+    loop(1, chips, ask)
+    sent.append(lambda: round_sent(sendid.at[pl.ds(0, others)], id_s.at[0]))
     idr[chip] = sendid[chip]
-    if MIXLATE:
-        dp_send_all(mixp, mixr, mix_s, mix_r)
+    if not MIXFIRST:
+        dp_round(mixp, mixr, mix_s, mix_r)
 
     def owner_at(j, q):
         return from_chip(j * GROUP + q + 1)
@@ -330,22 +329,32 @@
             pick_t[j, :, q * CAPL:(q + 1) * CAPL] = one_hot(iota((slots, CAPL), 0) == node)
             ksel_t[j, :, q * CAPL:(q + 1) * CAPL] = jnp.where(iota((8, CAPL), 0) == k, 1.0, 0.0)
 
+    used = pl.ds(0, CAP)
+
     def ask_group(j):
         got = lax.dot_general(pick_t[j], ng[...], (((0,), (0,)), ((), ())), preferred_element_type=F32)
         asked[j] = got.astype(BF16)
 
     def score(j, arrivals):
-        for q in range(arrivals):
-            wait_row(j * GROUP + q + 1)
+        round_got(rows_in.at[pl.ds(j * GROUP, arrivals), used], row_r.at[j])
         got = rows_in[j * GROUP:(j + 1) * GROUP].reshape(GROUP * CAPL, width).astype(F32)
         s = jnp.sum(got * asked[j].astype(F32), axis=1, keepdims=True)
         s = jnp.broadcast_to(s, (GROUP * CAPL, 128)).T[0:8, :]
+        zs[j] = s[0:1, :]
+        z_round(zs.at[j], zsr.at[j], zx_s.at[j], zx_r.at[j])
+        zsr[j, z] = zs[j]
+
+    def node_scores(j):
+        z_got(zsr.at[j], zx_r.at[j])
+        s = zsr[j, 0]
+        for i in range(1, nz):
+            s = s + zsr[j, i]
         s_hi = s.astype(BF16).astype(F32)
         by_k = jnp.concatenate([s_hi * ksel_t[j], (s - s_hi) * ksel_t[j]], axis=0).astype(BF16)
         return dot_nt(by_k, pick_t[j])
 
     def mix_in():
-        dp_wait_all(mixp, mixr, mix_s, mix_r)
+        dp_got(mixr, mix_r)
         for b in range(slots // step):
             rows = slice(b * step, (b + 1) * step)
             part = dot(live[0, rows, :], mixr[:, 0:pair_rows, :].reshape(slots, width)) + dot(
@@ -353,8 +362,6 @@
             )
             whole[z, rows, :] = part.astype(BF16)
 
-    if not MIXLATE:
-        mix_in()
     zright = lax.rem(z + 1, nz)
     zleft = lax.rem(z + nz - 1, nz)
 
@@ -387,9 +394,6 @@
         return b
 
     hops = nz // 2
-    if not MIXLATE:
-        ring_right(0).start()
-        ring_left(0).start()
     for j in range(groups):
         pick_group(j)
     scale = 1.0 / (float(full_rows) ** 0.5)
@@ -430,35 +434,27 @@
         rows_out[h, low:HALF, :] = (front[low:, :] + rear[:HALF - low, :]).astype(BF16)
         rows_out[h, HALF:CAP, :] = rear[HALF - low:, :].astype(BF16)
 
-    def row_copy(i):
+    def row_send(i):
         p = to_chip(i)
-        used = pl.ds(0, CAP)
-        return copy(
-            rows_out.at[p, used], rows_in.at[i - 1, used], row_s.at[p], row_r.at[i - 1], p * 2 + core, z
-        )
-
-    def wait_row(i):
-        p = from_chip(i)
-        used = pl.ds(0, CAP)
         copy(
-            rows_out.at[p, used], rows_in.at[i - 1, used], row_s.at[p], row_r.at[i - 1], p * 2 + core, z
-        ).wait_recv()
+            rows_out.at[p, used], rows_in.at[i - 1, used],
+            row_s.at[0], row_r.at[lax.div(i - 1, GROUP)], p * 2 + core, z,
+        ).start()
 
     def serve_far(i):
         h = to_chip(i)
-        chip_wait(sendid, idr, id_s, id_r, h)
+        round_got(idr.at[h], id_r.at[h])
         serve(h)
-        row_copy(i).start()
+        row_send(i)
 
     emb_copy(1 - core).wait_recv()
     fetch[2].wait()
     done = 1
-    if MIXLATE:
-        loop(done, 4, serve_far)
-        done = 4
-        mix_in()
-        ring_right(0).start()
-        ring_left(0).start()
+    loop(done, 4, serve_far)
+    done = 4
+    mix_in()
+    ring_right(0).start()
+    ring_left(0).start()
     use_block(z, True)
     for s in range(hops):
         upto = min(done + 5, chips)
@@ -478,7 +474,7 @@
         use_block(b)
     rows_in[chips - 1, 0:CAP, :] = rows_out[chip, 0:CAP, :]
     rows_in[:, CAP:CAPL, :] = jnp.zeros((chips, CAPL - CAP, width), BF16)
-    sent.append(lambda: loop(1, chips, lambda i: row_copy(i).wait_send()))
+    sent.append(lambda: round_sent(rows_out.at[pl.ds(0, others), used], row_s.at[0]))
     for s in range(hops):
         sent.append(functools.partial(lambda s: ring_right(s).wait_send(), s))
         sent.append(functools.partial(lambda s: ring_left(s).wait_send(), s))
@@ -488,36 +484,27 @@
     square = jnp.sum(hid * hid, axis=1, keepdims=True)
     ng[...] = (hid * gain).astype(BF16)
     square = jnp.broadcast_to(square, (slots, 128)).T[0:1, :]
+    folds = slots // 128
+    zq[...] = jnp.concatenate(
+        [square[:, f * 128:(f + 1) * 128] for f in range(folds)] + [jnp.zeros((8 - folds, 128), F32)], axis=0
+    )
+    z_round(zq, zqr, zq_s.at[0], zq_r.at[0])
+    zqr[z] = zq[...]
     for j in range(groups):
         ask_group(j)
-    got = score(0, GROUP)
+    for j in range(groups):
+        score(j, GROUP - (j + 1) // groups)
+
+    z_got(zqr, zq_r.at[0])
+    tot = zqr[0]
+    for i in range(1, nz):
+        tot = tot + zqr[i]
+    squares = jnp.concatenate([tot[f:f + 1, :] for f in range(folds)], axis=1)
+    recip = lax.rsqrt(squares / float(full_rows) + 1e-05)
+    got = node_scores(0)
     for j in range(1, groups):
-        got = got + score(j, GROUP - (j + 1) // groups)
-
-    zsend[:, 0:slots] = got[0:8, :] + got[8:16, :]
-    folds = slots // 128
-    zsend[:, slots:slots + 128] = jnp.concatenate(
-        [square[:, f * 128:(f + 1) * 128] for f in range(folds)] + [jnp.zeros((8 - folds, 128), F32)], axis=0
-    )
-
-    def zx(i):
-        zz = lax.rem(z + i, nz)
-        return copy(zsend, zr.at[z], zx_s.at[zz], zx_r.at[z], me, zz)
-
-    def zx_wait(i):
-        zz = lax.rem(z + i, nz)
-        copy(zsend, zr.at[zz], zx_s.at[zz], zx_r.at[zz], me, zz).wait_recv()
-
-    loop(1, nz, lambda i: zx(i).start())
-    sent.append(lambda: loop(1, nz, lambda i: zx(i).wait_send()))
-    zr[z] = zsend[...]
-    loop(1, nz, zx_wait)
-    tot = zr[0]
-    for i in range(1, nz):
-        tot = tot + zr[i]
-    raw = tot[:, 0:slots]
-    squares = jnp.concatenate([tot[f:f + 1, slots:slots + 128] for f in range(folds)], axis=1)
-    recip = lax.rsqrt(squares / float(full_rows) + 1e-05)
+        got = got + node_scores(j)
+    raw = got[0:8, :] + got[8:16, :]
     scores = raw * recip
     logp = scores - jnp.log(jnp.sum(jnp.exp(scores), axis=0, keepdims=True))
     prob = jnp.exp(logp)
@@ -557,30 +544,55 @@
         gown[q] = dot(whole_t[core * quarter + turn(q)], dh[...]) * scale
     per = chips // quarter
 
-    def rs_copy(p):
-        return chip_copy(rs_out, rs_in, rs_s, rs_r, p)
+    part_rows = width // per // CH
+
+    def rs_send(c, i, p):
+        copy(rs_out.at[c, p], rs_in.at[c, i], rs_s.at[c], rs_r.at[c], p * 2 + core, z).start()
+
+    batches = 3
+    batch = others // batches
+
+    def ag_send(c, i):
+        p = to_chip(i)
+        copy(
+            gfull.at[core, c, 0], gfull.at[core, c, i],
+            ag_s.at[c], ag_r.at[c * batches + lax.div(i - 1, batch)], p * 2 + core, z,
+        ).start()
+
+    def forward(c, b, side_core):
+        at = pl.ds(0, 1) if b == batches else pl.ds(1 + b * batch, batch)
+        ref = gfull.at[side_core, c, at]
+        n = c * (batches + 1) + b
+        return copy(ref, ref, fw_s.at[n], fw_r.at[n], sibling, z)
 
     for q in range(quarter):
         pair(q).wait_recv()
-        both = gown[q] + pair_in[q].astype(F32)
+        both = (gown[q] + pair_in[q].astype(F32)).astype(BF16).reshape(per, CH, part_rows, width)
         first = turn(q) * per
-        rs_out[pl.ds(first, per)] = both.astype(BF16).reshape(per, width // per, width)
+        for c in range(CH):
+            rs_out[c, pl.ds(first, per)] = both[:, c]
         for i in range(1 if q == 0 else 0, per):
-            rs_copy(first + lax.rem(chip_x + i, per)).start()
+            rs_send(0, q * per + i, first + lax.rem(chip_x + i, per))
+    for c in range(1, CH):
+        loop(1, chips, lambda i: rs_send(c, i, to_chip(i)))
     for q in range(quarter):
         sent.append(functools.partial(lambda q: pair(q).wait_send(), q))
-
-    def chip_got(src, dst, ss, rs):
-        loop(1, chips, lambda i: chip_wait(src, dst, ss, rs, from_chip(i)))
-
-    sent.append(lambda: chip_sent_all(rs_out, rs_in, rs_s, rs_r))
-    rs_in[chip] = rs_out[chip]
-    chip_got(rs_out, rs_in, rs_s, rs_r)
-    shard = rs_in[0].astype(F32)
-    for p in range(1, chips):
-        shard = shard + rs_in[p].astype(F32)
-    gfull[core, chip] = shard.astype(BF16)
-    energy = jnp.sum(jnp.sum(shard * shard, axis=1, keepdims=True), axis=0, keepdims=True)
+    for c in range(CH):
+        sent.append(functools.partial(lambda c: round_sent(rs_out.at[c, pl.ds(0, others)], rs_s.at[c]), c))
+        sent.append(functools.partial(lambda c: round_sent(gfull.at[core, c, pl.ds(0, others)], ag_s.at[c]), c))
+        for b in range(batches + 1):
+            sent.append(functools.partial(lambda c, b: forward(c, b, core).wait_send(), c, b))
+    energy = jnp.zeros((1, 1), F32)
+    for c in range(CH):
+        rs_in[c, 0] = rs_out[c, chip]
+        round_got(rs_in.at[c, pl.ds(1, others)], rs_r.at[c])
+        shard = rs_in[c, 0].astype(F32)
+        for p in range(1, chips):
+            shard = shard + rs_in[c, p].astype(F32)
+        gfull[core, c, 0] = shard.astype(BF16)
+        energy = energy + jnp.sum(jnp.sum(shard * shard, axis=1, keepdims=True), axis=0, keepdims=True)
+        loop(1, chips, lambda i: ag_send(c, i))
+        forward(c, batches, core).start()
     row = iota((8, 128), 0)
     tile = jnp.where(row == 0, energy, jnp.where(row == 1, num, jnp.where(row == 2, den, over)))
 
@@ -588,66 +600,34 @@
     both_cores = copy(sb_out, sb, sb_s.at[0], sb_r.at[0], sibling, z)
     both_cores.start()
 
-    def ezc(i):
-        zz = lax.rem(z + i, nz)
-        return copy(ez_out, ez.at[z], ez_s.at[zz], ez_r.at[z], me, zz)
-
-    def ezc_wait(i):
-        zz = lax.rem(z + i, nz)
-        copy(ez_out, ez.at[zz], ez_s.at[zz], ez_r.at[zz], me, zz).wait_recv()
-
-    def ag(i):
-        p = to_chip(i)
-        return copy(gfull.at[core, chip], gfull.at[core, chip], ag_s.at[p], ag_r.at[chip], p * 2 + core, z)
-
-    def ag_wait(i):
-        p = from_chip(i)
-        copy(gfull.at[core, p], gfull.at[core, p], ag_s.at[p], ag_r.at[p], p * 2 + core, z).wait_recv()
-        return p
-
-    def forward(p):
-        return copy(gfull.at[core, p], gfull.at[core, p], fw_s.at[p], fw_r.at[p], sibling, z)
-
-    def forward_wait(p):
-        copy(gfull.at[1 - core, p], gfull.at[1 - core, p], fw_s.at[p], fw_r.at[p], sibling, z).wait_recv()
-
     sent.append(both_cores.wait_send)
-    sent.append(lambda: loop(1, nz, lambda i: ezc(i).wait_send()))
-    sent.append(lambda: loop(1, chips, lambda i: ag(i).wait_send()))
-    sent.append(lambda: loop(0, chips, lambda p: forward(p).wait_send()))
-
-    loop(1, chips, lambda i: ag(i).start())
-    forward(chip).start()
+
+    def ag_pass(c, b):
+        round_got(gfull.at[core, c, pl.ds(1 + b * batch, batch)], ag_r.at[c * batches + b])
+        forward(c, b, core).start()
+
     both_cores.wait_recv()
     tile = tile + sb[...]
     ez_out[...] = tile
-    loop(1, nz, lambda i: ezc(i).start())
+    z_round(ez_out, ez, ez_s.at[0], ez_r.at[0])
     ez[z] = tile
-    loop(1, nz, ezc_wait)
+    z_got(ez, ez_r.at[0])
     etot = ez[0]
     for i in range(1, nz):
         etot = etot + ez[i]
     tile = jnp.where(row == 0, etot, tile)
     dt_out[...] = tile
 
-    def dtc(i):
-        p = to_chip(i)
-        return copy(dt_out, dt.at[chip], dt_s.at[p], dt_r.at[chip], p * 2 + core, z)
-
-    def dtc_wait(i):
-        p = from_chip(i)
-        copy(dt_out, dt.at[p], dt_s.at[p], dt_r.at[p], p * 2 + core, z).wait_recv()
-
-    loop(1, chips, lambda i: dtc(i).start())
-    sent.append(lambda: loop(1, chips, lambda i: dtc(i).wait_send()))
-    dt[chip] = tile
-
-    def ag_pass(i):
-        p = ag_wait(i)
-        forward(p).start()
-
-    loop(1, chips, ag_pass)
-    loop(1, chips, dtc_wait)
+    def tell(i):
+        copy(dt_out, dt.at[i], dt_s.at[0], dt_r.at[0], to_chip(i) * 2 + core, z).start()
+
+    loop(1, chips, tell)
+    sent.append(lambda: round_sent(dt.at[pl.ds(1, others)], dt_s.at[0]))
+    dt[0] = tile
+    for c in range(CH):
+        for b in range(batches):
+            ag_pass(c, b)
+    round_got(dt.at[pl.ds(1, others)], dt_r.at[0])
     total = dt[0]
     for i in range(1, chips):
         total = total + dt[i]
@@ -658,17 +638,17 @@
 
     blk_rows = width // per
 
-    def finish(h, p):
-        r = pl.ds(pl.multiple_of((h * chips + p) * blk_rows, blk_rows), blk_rows)
-        out[r, :] = (proj[r, :].astype(F32) - gfull[h, p].astype(F32) * factor).astype(BF16)
-
-    loop(0, chips, lambda p: finish(core, p))
-
-    def finish_far(p):
-        forward_wait(p)
-        finish(1 - core, p)
-
-    loop(0, chips, finish_far)
+    def finish(h, c, i, p):
+        at = (h * chips + p) * blk_rows + c * part_rows
+        r = pl.ds(pl.multiple_of(at, part_rows), part_rows)
+        out[r, :] = (proj[r, :].astype(F32) - gfull[h, c, i].astype(F32) * factor).astype(BF16)
+
+    for c in range(CH):
+        loop(0, chips, lambda i: finish(core, c, i, from_chip(i)))
+    for c in range(CH):
+        for b in range(batches, -1, -1):
+            forward(c, b, 1 - core).wait_recv()
+        loop(0, chips, lambda i: finish(1 - core, c, i, from_chip(i, True)))
 
     for wait in sent:
         wait()
@@ -711,16 +691,17 @@
         vm((chips // GROUP, slots, GROUP * CAPL), BF16),
         vm((chips // GROUP, 8, GROUP * CAPL), F32),
         vm((chips // GROUP, GROUP * CAPL, width), BF16),
-        vm((16, slots), F32),
-        vm((8, slots + 128), F32),
-        vm((nz, 8, slots + 128), F32),
+        vm((8, 128), F32),
+        vm((nz, 8, 128), F32),
+        vm((chips // GROUP, 1, GROUP * CAPL), F32),
+        vm((chips // GROUP, nz, 1, GROUP * CAPL), F32),
         vm((slots, width), BF16),
         vm((quarter, width, width), BF16),
         vm((quarter, width, width), BF16),
         vm((quarter, width, width), F32),
-        vm((chips, width // per, width), BF16),
-        vm((chips, width // per, width), BF16),
-        vm((2, chips, width // per, width), BF16),
+        vm((CH, chips, width // per // CH, width), BF16),
+        vm((CH, chips, width // per // CH, width), BF16),
+        vm((2, CH, chips, width // per // CH, width), BF16),
         vm((8, 128), F32),
         vm((8, 128), F32),
         vm((8, 128), F32),
@@ -730,9 +711,9 @@
     ]
     dma = pltpu.SemaphoreType.DMA
     for count in (
-        2, 2, nd, nd, nd, nd, chips, chips, chips, chips,
-        nz, nz, nz, nz, nz, nz, quarter, quarter,
-        chips, chips, chips, chips, chips, chips, 1, 1, nz, nz, chips, chips,
+        2, 2, 1, 1, 1, 1, 1, chips, 1, chips // GROUP,
+        nz, nz, nz, nz, chips // GROUP, chips // GROUP, 1, 1, quarter, quarter,
+        CH, CH, CH, 3 * CH, 4 * CH, 4 * CH, 1, 1, 1, 1, 1, 1,
     ):
         scratch.append(dma((count,)))
     in_vmem = pl.BlockSpec(memory_space=pltpu.VMEM)

time: 108 us -> 99.6 us (0.922)
  Pallas kernels: 104 us -> 95.2 us
    pallas_call x1, Pallas kernels: 104 us -> 95.2 us  [fast_step(): pl.pallas_call(functools.partial(step_kernel, nd, nz, full_rows), out_sha...]
where the time goes in v2:
time: 99.6 us; the launch traced here: 99.5 us
  Pallas kernels  95.2 us (96%)
  between operations  3.03 us (3%)
    pallas_call x1, Pallas kernels, fast_step(): pl.pallas_call(functools.partial(step_kernel, nd, nz, full_rows), out_sha...  95.2 us

profile of v2, /device:TPU:1, one launch (start us, length us, event | category | flops | bytes accessed | tf_op | source)
XLA Modules:
  0.0 99.5 jit_solution(9205320037378658138)
XLA Ops:
  0.6 95.2 %step.1 = (bf16[2048,256]{1,0:T(8,128)(2,1)S(1)}, f32[1,1]{1,0:T(1,128)}, f32[1,1]{1,0:T(1,128)}) custom-call(s32[32]{0:T(128)} %counts.1, s32[8,1024]{1,0:T(8,128)} %bitcast.41, bf16[8,1024]{1,0:T(8,128)(2,1)} %bitcast.39, s32[8,128]{1,0:T(8,128)} %bitcast.45, s32[8,128]{1,0:T(8,128)} %bitcast.44, bf16[2,128]{1,0:T(2,128)(2,1)} %bitcast.47, ...), custom_call_target="tpu_custom_call" | custom-call | tf_op jit(solution)/shard_map/step/pallas_call | solution.py:720
  96.5 0.3 conditional.1
  96.8 1.0 copy.53
